TPU v7x, 256 devices: a whole 4x4x8 slice. The times are simulated.
256 devices in a mesh: spin: 2 (over core), dom: 128 (over x, z, y).
Axes of the slice: x: 4, y: 4, z: 8, core: 2. Of those that a mesh axis runs over, the one named last changes fastest.
Arguments:
- orbitals: bfloat16 [512, 2048, 128], P(('spin', 'dom')), parts along dimension 0, may hold values from -240 to 240
- potential: float32 [4096, 8, 128], P(('spin', 'dom')), parts along dimension 0, may hold values from -7 to 7
- cutoff: float32 [2], P('spin'), parts along dimension 0, may hold values from 3 to 9
- ceiling: float32 [2], P('spin'), parts along dimension 0, may hold values from 44 to 52
Outputs:
- rotated: bfloat16 [512, 2048, 128], P(('spin', 'dom')), parts along dimension 0
- projected: float32 [64, 32], P('spin'), parts along dimension 0
There are 2 independent parts, one for each index of `spin`. A program takes and returns all parts, laid end to end along the dimension named above; each array names one. Nothing has to cross between parts.
All inputs are finite; a program needn't handle non-finite values.
Results may differ from a plain program's by a relative error of at most 0.0045.
Values may be sent and summed in bfloat16 or wider, within the bound.
No kernel may reach another device: no remote copies, remote signals or barrier semaphores. Data moves between devices by JAX's collectives and lax.ppermute only.
A program may use at most 64 MiB of HBM per device.

v0:
```python
import jax
import jax.numpy as jnp
from jax import lax
from jax.sharding import PartitionSpec as P

DEGREE = 3


STENCIL = (
    -5369.0 / 1800.0,
    12.0 / 7.0,
    -15.0 / 56.0,
    10.0 / 189.0,
    -1.0 / 112.0,
    2.0 / 1925.0,
    -1.0 / 16632.0,
)
KINETIC = -2.0


def with_halo(cells, sides, width):
    for axis, dim in sides:
        count = lax.axis_size(axis)
        ends = count - 1
        head = lax.slice_in_dim(cells, 0, width, axis=dim)
        tail = lax.slice_in_dim(cells, cells.shape[dim] - width, cells.shape[dim], axis=dim)
        cells = jnp.concatenate(
            [
                lax.ppermute(tail, axis, [(i, (i + 1) % count) for i in range(ends)]),
                cells,
                lax.ppermute(head, axis, [((i + 1) % count, i) for i in range(ends)]),
            ],
            axis=dim,
        )
    return cells


def inner_products(left, right):
    return jnp.dot(
        left, right.T, precision=lax.Precision.HIGHEST, preferred_element_type=jnp.float32
    )


def stencil_apply(padded, potential_yx):
    band_count, y_cells, wide_planes, z_cells = padded.shape
    x_planes = wide_planes - 12
    field = padded[:, :, 6 : 6 + x_planes, :]
    widened = jnp.pad(field, ((0, 0), (6, 6), (0, 0), (6, 6)))
    laplace = 3.0 * STENCIL[0] * field
    for offset in range(1, 7):
        weight = STENCIL[offset]
        upper = 6 + offset
        lower = 6 - offset
        laplace = laplace + weight * (
            padded[:, :, upper : upper + x_planes, :] + padded[:, :, lower : lower + x_planes, :]
        )
        laplace = laplace + weight * (
            widened[:, upper : upper + y_cells, :, 6 : 6 + z_cells]
            + widened[:, lower : lower + y_cells, :, 6 : 6 + z_cells]
        )
        laplace = laplace + weight * (
            widened[:, 6 : 6 + y_cells, :, upper : upper + z_cells]
            + widened[:, 6 : 6 + y_cells, :, lower : lower + z_cells]
        )
    return KINETIC * laplace + potential_yx * field


def apply_hamiltonian(field, potential_yx):
    padded = with_halo(field, (("dom", 2),), 6)
    return stencil_apply(padded, potential_yx)


def local(orbitals, potential, cutoff, ceiling):
    x_cells = orbitals.shape[1]
    z_cells = orbitals.shape[2]
    y_cells = potential.shape[1]
    slab_rows = lax.all_to_all(orbitals, "dom", split_axis=1, concat_axis=0, tiled=True)
    x_planes = slab_rows.shape[1]
    band_count = slab_rows.shape[0] // y_cells
    start = slab_rows.reshape(band_count, y_cells, x_planes, z_cells).astype(jnp.float32)
    potential_yx = jnp.swapaxes(potential, 0, 1)
    center = 0.5 * (ceiling[0] + cutoff[0])
    half_width = 0.5 * (ceiling[0] - cutoff[0])
    previous = start
    current = (apply_hamiltonian(start, potential_yx) - center * start) / half_width
    for repeat in range(DEGREE - 1):
        upcoming = (
            2.0 * (apply_hamiltonian(current, potential_yx) - center * current) / half_width
            - previous
        )
        previous, current = (current, upcoming)
    ham_image = None
    cell_count = x_cells * y_cells * z_cells
    flattened = current.reshape(band_count, y_cells * x_planes * z_cells)
    gram_part = inner_products(flattened, flattened)
    gram_total = lax.psum(gram_part, "dom")
    ham_image = apply_hamiltonian(current, potential_yx)
    mixed_part = inner_products(
        flattened, ham_image.reshape(band_count, y_cells * x_planes * z_cells)
    )
    mixed_total = lax.psum(mixed_part, "dom")
    gram_total = gram_total / cell_count
    mixed_total = mixed_total / cell_count
    subspace_ham = 0.5 * (mixed_total + mixed_total.T)
    factor = jnp.linalg.cholesky(gram_total)
    inverse = jax.scipy.linalg.solve_triangular(
        factor, jnp.eye(band_count, dtype=jnp.float32), lower=True
    )
    rotated = jnp.dot(
        inverse, flattened, precision=lax.Precision.HIGHEST, preferred_element_type=jnp.float32
    )
    rotated = rotated.astype(jnp.bfloat16).reshape(band_count * y_cells, x_planes, z_cells)
    returned = lax.all_to_all(rotated, "dom", split_axis=0, concat_axis=1, tiled=True)
    left_part = jnp.dot(
        inverse, subspace_ham, precision=lax.Precision.HIGHEST, preferred_element_type=jnp.float32
    )
    projected = jnp.dot(
        left_part, inverse.T, precision=lax.Precision.HIGHEST, preferred_element_type=jnp.float32
    )
    return (returned, projected)


def solution(mesh):
    return jax.shard_map(
        local,
        mesh=mesh,
        in_specs=(
            P(("spin", "dom"), None, None),
            P(("spin", "dom"), None, None),
            P("spin"),
            P("spin"),
        ),
        out_specs=(P(("spin", "dom"), None, None), P("spin", None)),
        check_vma=False,
    )
```

profile of v0, /device:TPU:2, one launch (start us, length us, event | category | flops | bytes accessed | tf_op | source)
XLA Modules:
  0.0 907.7 jit_solution(11817646819286451613)
XLA Ops:
  0.6 2.8 copy.36
  3.5 44.8 %all_to_all.27 = bf16[2,2048,128]{2,0,1:T(2,128)(2,1)S(1)} all-to-all(bf16[2,2048,128]{2,0,1:T(2,128)(2,1)S(1)} %copy.36), channel_id=1, replica_groups=mesh['spin'=2,'dom'=128] {'dom'}, dimensions={1} | all-to-all | bytes 2097152 | tf_op jit(solution)/shard_map/all_to_all | solution.py:77
  48.6 0.2 copy.38
  48.8 0.3 fusion.300
  49.3 2.3 collective-permute-start.1
  51.8 7.8 collective-permute-start
  60.9 11.0 %collective-permute-done.1 = f32[32,8,6,128]{3,1,2,0:T(8,128)S(1)} collective-permute-done((f32[32,8,6,128]{3,1,2,0:T(8,128)S(1)}, f32[32,8,6,128]{3,1,2,0:T(8,128)S(1)}, u32[]{:S(2)}, u32[]{:S(2)}) %collective-permute-start.1) | collective-permute-done | bytes 786464 | tf_op jit(solution)/shard_map/ppermute | solution.py:29
  71.9 0.2 copy.42
  72.1 1.1 collective-permute-done
  73.2 0.2 copy.40
  73.4 8.5 fusion.138
  82.0 0.3 fusion.299
  82.4 1.9 collective-permute-start.3
  84.5 8.6 collective-permute-start.2
  93.1 11.4 %collective-permute-done.3 = f32[32,8,6,128]{3,1,2,0:T(8,128)S(1)} collective-permute-done((f32[32,8,6,128]{3,1,2,0:T(8,128)S(1)}, f32[32,8,6,128]{3,1,2,0:T(8,128)S(1)}, u32[]{:S(2)}, u32[]{:S(2)}) %collective-permute-start.3) | collective-permute-done | bytes 786464 | tf_op jit(solution)/shard_map/ppermute | solution.py:29
  104.5 0.2 copy.47
  104.7 1.1 collective-permute-done.2
  105.8 1.2 copy.45
  107.0 10.8 %fusion.276 = f32[32,8,16,128]{3,2,1,0:T(8,128)S(1)} fusion(f32[32,8,16,128]{3,2,1,0:T(8,128)S(1)} %fusion.138, f32[32,8,6,128]{3,2,1,0:T(8,128)S(1)} %copy.47, f32[32,8,6,128]{3,2,1,0:T(8,128)} %copy.45, f32[]{:T(128)} %bitcast.5, f32[]{:T(128)} %bitcast.4, f32[8,16,128]{2,1,0:T(8,128)S(1)} %copy.43, f32[32,8,16,128]{3,2,1,0:T(8,128)S(1)} %bitcast.42), kind=kLoop, calls=%fused_computation.462 | loop fusion | flops 39321600 | bytes 7929864 | tf_op jit(solution)/shard_map/sub | solution.py:88
  118.0 1.1 copy-done
  119.3 1.9 collective-permute-start.5
  121.4 8.9 collective-permute-start.4
  130.3 10.2 %collective-permute-done.5 = f32[32,8,6,128]{3,1,2,0:T(8,128)S(1)} collective-permute-done((f32[32,8,6,128]{3,1,2,0:T(8,128)S(1)}, f32[32,8,6,128]{3,1,2,0:T(8,128)S(1)}, u32[]{:S(2)}, u32[]{:S(2)}) %collective-permute-start.5) | collective-permute-done | bytes 786464 | tf_op jit(solution)/shard_map/ppermute | solution.py:29
  140.5 0.2 copy.51
  140.7 1.3 collective-permute-done.4
  141.9 1.2 copy.49
  143.1 10.8 %fusion.277 = f32[32,8,16,128]{3,2,1,0:T(8,128)S(1)} fusion(f32[32,8,16,128]{3,2,1,0:T(8,128)S(1)} %fusion.138, f32[32,8,16,128]{3,2,1,0:T(8,128)S(1)} %copy-done.1, f32[32,8,6,128]{3,2,1,0:T(8,128)S(1)} %copy.51, f32[32,8,6,128]{3,2,1,0:T(8,128)} %copy.49, f32[]{:T(128)} %bitcast.5, f32[]{:T(128)} %bitcast.4, f32[8,16,128]{2,1,0:T(8,128)S(1)} %copy.43), kind=kLoop, calls=%fused_computation.463 | loop fusion | flops 39321600 | bytes 7929864 | tf_op jit(solution)/shard_map/sub | solution.py:88
  153.9 0.3 fusion.297
  154.3 1.9 collective-permute-start.7
  156.4 8.6 collective-permute-start.6
  165.0 2.8 fusion.281
  167.9 6.7 collective-permute-done.7
  174.8 1.1 collective-permute-done.6
  175.9 0.2 copy.59
  176.1 8.2 fusion.10
  184.4 4.0 fusion.284
  188.4 611.8 %all-reduce.4 = (f32[32,32]{0,1:T(8,128)S(1)}, f32[32,32]{0,1:T(8,128)S(1)}) all-reduce(f32[32,32]{0,1:T(8,128)S(1)} %fusion.281, f32[32,32]{0,1:T(8,128)S(1)} %fusion.284), channel_id=1, replica_groups=mesh['spin'=2,'dom'=128] {'dom'}, use_global_device_ids=true, to_apply=%region_0.1 | all-reduce | flops 2048 | bytes 16384 | tf_op jit(solution)/shard_map/psum | solution.py:96
  800.4 2.9 cholesky.17
  803.4 0.6 compare_reduce_fusion
  804.0 0.7 fusion.289
  804.7 2.4 custom-call.7
  807.1 0.2 fusion.293
  807.3 3.0 convolution_convert_fusion
  810.3 1.3 reshape.35
  811.6 75.0 %all-to-all-start.1 = ((bf16[256,16,128]{2,1,0:T(8,128)(2,1)}), bf16[256,16,128]{2,1,0:T(8,128)(2,1)S(1)}, u32[]{:S(2)}, u32[]{:S(2)}) async-start(bf16[256,16,128]{2,1,0:T(8,128)(2,1)} %reshape.35), calls=%async_computation.1 | async-start | bytes 2097152 | tf_op jit(solution)/shard_map/all_to_all | solution.py:113
  886.9 0.8 fusion.301
  887.6 18.9 %all-to-all-done.1 = bf16[256,16,128]{2,1,0:T(8,128)(2,1)S(1)} async-done(((bf16[256,16,128]{2,1,0:T(8,128)(2,1)}), bf16[256,16,128]{2,1,0:T(8,128)(2,1)S(1)}, u32[]{:S(2)}, u32[]{:S(2)}) %all-to-all-start.1) | async-done | bytes 1048608 | tf_op jit(solution)/shard_map/all_to_all | solution.py:113
  906.6 1.1 copy.57
  (26 shorter events, 2.3 us)
Async XLA Ops:
  49.1 11.7 %copy-start.2 = (f32[16,8,128]{2,1,0:T(8,128)S(1)}, f32[16,8,128]{2,1,0:T(8,128)}, u32[]{:S(2)}) copy-start(f32[16,8,128]{2,1,0:T(8,128)} %param.5) | copy-start | bytes 196612
  49.3 22.6 %collective-permute-start.1 = (f32[32,8,6,128]{3,1,2,0:T(8,128)S(1)}, f32[32,8,6,128]{3,1,2,0:T(8,128)S(1)}, u32[]{:S(2)}, u32[]{:S(2)}) collective-permute-start(f32[32,8,6,128]{3,1,2,0:T(8,128)S(1)} %copy.41), channel_id=1, source_target_pairs={{0,1},{1,2},{2,3},{3,4},{4,5},{5,6},{6,7},{7,8},{8,9},{9,10},{10,1... | collective-permute-start | bytes 2359304 | tf_op jit(solution)/shard_map/ppermute | solution.py:29
  51.8 21.4 %collective-permute-start = (f32[32,8,6,128]{3,1,2,0:T(8,128)S(1)}, f32[32,8,6,128]{3,1,2,0:T(8,128)S(1)}, u32[]{:S(2)}, u32[]{:S(2)}) collective-permute-start(f32[32,8,6,128]{3,1,2,0:T(8,128)S(1)} %copy.39), channel_id=1, source_target_pairs={{1,0},{2,1},{3,2},{4,3},{5,4},{6,5},{7,6},{8,7},{9,8},{10,9},{11,1... | collective-permute-start | bytes 2359304 | tf_op jit(solution)/shard_map/ppermute | solution.py:31
  82.4 22.1 %collective-permute-start.3 = (f32[32,8,6,128]{3,1,2,0:T(8,128)S(1)}, f32[32,8,6,128]{3,1,2,0:T(8,128)S(1)}, u32[]{:S(2)}, u32[]{:S(2)}) collective-permute-start(f32[32,8,6,128]{3,1,2,0:T(8,128)S(1)} %copy.46), channel_id=1, source_target_pairs={{0,1},{1,2},{2,3},{3,4},{4,5},{5,6},{6,7},{7,8},{8,9},{9,10},{10,1... | collective-permute-start | bytes 2359304 | tf_op jit(solution)/shard_map/ppermute | solution.py:29
  84.5 21.4 %collective-permute-start.2 = (f32[32,8,6,128]{3,1,2,0:T(8,128)S(1)}, f32[32,8,6,128]{3,1,2,0:T(8,128)S(1)}, u32[]{:S(2)}, u32[]{:S(2)}) collective-permute-start(f32[32,8,6,128]{3,1,2,0:T(8,128)S(1)} %copy.44), channel_id=1, source_target_pairs={{1,0},{2,1},{3,2},{4,3},{5,4},{6,5},{7,6},{8,7},{9,8},{10,9},{11,1... | collective-permute-start | bytes 2359304 | tf_op jit(solution)/shard_map/ppermute | solution.py:31
  117.8 1.3 copy-start
  119.3 21.2 %collective-permute-start.5 = (f32[32,8,6,128]{3,1,2,0:T(8,128)S(1)}, f32[32,8,6,128]{3,1,2,0:T(8,128)S(1)}, u32[]{:S(2)}, u32[]{:S(2)}) collective-permute-start(f32[32,8,6,128]{3,1,2,0:T(8,128)S(1)} %copy.50), channel_id=1, source_target_pairs={{0,1},{1,2},{2,3},{3,4},{4,5},{5,6},{6,7},{7,8},{8,9},{9,10},{10,1... | collective-permute-start | bytes 2359304 | tf_op jit(solution)/shard_map/ppermute | solution.py:29
  121.4 21.8 %copy-start.1 = (f32[32,8,16,128]{3,2,1,0:T(8,128)S(1)}, f32[32,8,16,128]{3,2,1,0:T(8,128)}, u32[]{:S(2)}) copy-start(f32[32,8,16,128]{3,2,1,0:T(8,128)} %copy-done) | copy-start | bytes 6291460
  121.4 20.6 %collective-permute-start.4 = (f32[32,8,6,128]{3,1,2,0:T(8,128)S(1)}, f32[32,8,6,128]{3,1,2,0:T(8,128)S(1)}, u32[]{:S(2)}, u32[]{:S(2)}) collective-permute-start(f32[32,8,6,128]{3,1,2,0:T(8,128)S(1)} %copy.48), channel_id=1, source_target_pairs={{1,0},{2,1},{3,2},{4,3},{5,4},{6,5},{7,6},{8,7},{9,8},{10,9},{11,1... | collective-permute-start | bytes 2359304 | tf_op jit(solution)/shard_map/ppermute | solution.py:31
  154.3 20.3 %collective-permute-start.7 = (f32[32,8,6,128]{3,1,2,0:T(8,128)S(1)}, f32[32,8,6,128]{3,1,2,0:T(8,128)S(1)}, u32[]{:S(2)}, u32[]{:S(2)}) collective-permute-start(f32[32,8,6,128]{3,1,2,0:T(8,128)S(1)} %copy.60), channel_id=1, source_target_pairs={{0,1},{1,2},{2,3},{3,4},{4,5},{5,6},{6,7},{7,8},{8,9},{9,10},{10,1... | collective-permute-start | bytes 2359304 | tf_op jit(solution)/shard_map/ppermute | solution.py:29
  156.4 19.5 %collective-permute-start.6 = (f32[32,8,6,128]{3,1,2,0:T(8,128)S(1)}, f32[32,8,6,128]{3,1,2,0:T(8,128)S(1)}, u32[]{:S(2)}, u32[]{:S(2)}) collective-permute-start(f32[32,8,6,128]{3,1,2,0:T(8,128)S(1)} %copy.58), channel_id=1, source_target_pairs={{1,0},{2,1},{3,2},{4,3},{5,4},{6,5},{7,6},{8,7},{9,8},{10,9},{11,1... | collective-permute-start | bytes 2359304 | tf_op jit(solution)/shard_map/ppermute | solution.py:31
  811.6 94.9 %all-to-all-start.1 = ((bf16[256,16,128]{2,1,0:T(8,128)(2,1)}), bf16[256,16,128]{2,1,0:T(8,128)(2,1)S(1)}, u32[]{:S(2)}, u32[]{:S(2)}) async-start(bf16[256,16,128]{2,1,0:T(8,128)(2,1)} %reshape.35), calls=%async_computation.1 | async-start | bytes 2097152 | tf_op jit(solution)/shard_map/all_to_all | solution.py:113
where the time goes:
time: 908 us
  blocking collectives  657 us (72%)
  starting transfers between devices  117 us (13%)
  waiting for transfers between devices  62.9 us (7%)
  other arithmetic  45.2 us (5%)
  local copies, waits for them, and re-layouts  12.9 us (1%)
  matrix products  11 us (1%)
    psum x1, blocking collectives, local(): gram_total = lax.psum(gram_part, 'dom')  612 us
    all_to_all x1, starting transfers between devices, local(): lax.all_to_all(rotated, 'dom', split_axis=0, concat_axis=1, tiled=True)  75 us
    all_to_all x1, blocking collectives, local(): lax.all_to_all(orbitals, 'dom', split_axis=1, concat_axis=0, tiled=True)  44.8 us
    ppermute x4, waiting for transfers between devices, with_halo(): lax.ppermute(tail, axis, [(i, (i + 1) % count) for i in range(ends)])  39.3 us
    ppermute x4, starting transfers between devices, with_halo(): lax.ppermute(head, axis, [((i + 1) % count, i) for i in range(ends)])  33.9 us
    sub x2, other arithmetic, local(): 2.0 * (apply_hamiltonian(current, potential_yx) - center * current)  21.5 us
    all_to_all x1, waiting for transfers between devices, local(): lax.all_to_all(rotated, 'dom', split_axis=0, concat_axis=1, tiled=True)  18.9 us
  transfers between devices with their start and end apart: 9, of which 9 were waited for; matrix products, arithmetic and copies ran while one was open for 1% of the time, Pallas kernels for 0%

commit v1 on v0

--- a/solution.py
+++ b/solution.py
@@ -1,9 +1,10 @@
 import jax
 import jax.numpy as jnp
 from jax import lax
-from jax.sharding import PartitionSpec as P
+from jax.sharding import Mesh, PartitionSpec as P
 
 DEGREE = 3
+DOM = ("x", "z", "y")
 
 
 STENCIL = (
@@ -22,17 +23,23 @@
     for axis, dim in sides:
         count = lax.axis_size(axis)
         ends = count - 1
-        head = lax.slice_in_dim(cells, 0, width, axis=dim)
+        head = lax.slice_in_dim(cells, 0, width, axis=dim).astype(jnp.bfloat16)
         tail = lax.slice_in_dim(cells, cells.shape[dim] - width, cells.shape[dim], axis=dim)
+        tail = tail.astype(jnp.bfloat16)
+        lower = lax.ppermute(tail, axis, [(i, (i + 1) % count) for i in range(ends)])
+        upper = lax.ppermute(head, axis, [((i + 1) % count, i) for i in range(ends)])
         cells = jnp.concatenate(
-            [
-                lax.ppermute(tail, axis, [(i, (i + 1) % count) for i in range(ends)]),
-                cells,
-                lax.ppermute(head, axis, [((i + 1) % count, i) for i in range(ends)]),
-            ],
-            axis=dim,
+            [lower.astype(cells.dtype), cells, upper.astype(cells.dtype)], axis=dim
         )
     return cells
+
+
+def sum_over(value, axes):
+    count = 1
+    for axis in axes:
+        count *= lax.axis_size(axis)
+    copies = jnp.broadcast_to(value[None], (count,) + value.shape)
+    return jnp.sum(lax.all_to_all(copies, axes, split_axis=0, concat_axis=0, tiled=True), axis=0)
 
 
 def inner_products(left, right):
@@ -66,7 +73,7 @@
 
 
 def apply_hamiltonian(field, potential_yx):
-    padded = with_halo(field, (("dom", 2),), 6)
+    padded = with_halo(field, ((DOM, 2),), 6)
     return stencil_apply(padded, potential_yx)
 
 
@@ -74,7 +81,7 @@
     x_cells = orbitals.shape[1]
     z_cells = orbitals.shape[2]
     y_cells = potential.shape[1]
-    slab_rows = lax.all_to_all(orbitals, "dom", split_axis=1, concat_axis=0, tiled=True)
+    slab_rows = lax.all_to_all(orbitals, DOM, split_axis=1, concat_axis=0, tiled=True)
     x_planes = slab_rows.shape[1]
     band_count = slab_rows.shape[0] // y_cells
     start = slab_rows.reshape(band_count, y_cells, x_planes, z_cells).astype(jnp.float32)
@@ -93,12 +100,13 @@
     cell_count = x_cells * y_cells * z_cells
     flattened = current.reshape(band_count, y_cells * x_planes * z_cells)
     gram_part = inner_products(flattened, flattened)
-    gram_total = lax.psum(gram_part, "dom")
     ham_image = apply_hamiltonian(current, potential_yx)
     mixed_part = inner_products(
         flattened, ham_image.reshape(band_count, y_cells * x_planes * z_cells)
     )
-    mixed_total = lax.psum(mixed_part, "dom")
+    totals = jnp.concatenate([gram_part, mixed_part], axis=0).reshape(16, 128)
+    totals = sum_over(sum_over(totals, ("x", "y")), ("z",)).reshape(2 * band_count, band_count)
+    gram_total, mixed_total = totals[:band_count], totals[band_count:]
     gram_total = gram_total / cell_count
     mixed_total = mixed_total / cell_count
     subspace_ham = 0.5 * (mixed_total + mixed_total.T)
@@ -110,7 +118,7 @@
         inverse, flattened, precision=lax.Precision.HIGHEST, preferred_element_type=jnp.float32
     )
     rotated = rotated.astype(jnp.bfloat16).reshape(band_count * y_cells, x_planes, z_cells)
-    returned = lax.all_to_all(rotated, "dom", split_axis=0, concat_axis=1, tiled=True)
+    returned = lax.all_to_all(rotated, DOM, split_axis=0, concat_axis=1, tiled=True)
     left_part = jnp.dot(
         inverse, subspace_ham, precision=lax.Precision.HIGHEST, preferred_element_type=jnp.float32
     )
@@ -121,15 +129,16 @@
 
 
 def solution(mesh):
+    mesh = Mesh(mesh.devices.reshape(2, 4, 8, 4), ("spin",) + DOM)
     return jax.shard_map(
         local,
         mesh=mesh,
         in_specs=(
-            P(("spin", "dom"), None, None),
-            P(("spin", "dom"), None, None),
+            P(("spin",) + DOM, None, None),
+            P(("spin",) + DOM, None, None),
             P("spin"),
             P("spin"),
         ),
-        out_specs=(P(("spin", "dom"), None, None), P("spin", None)),
+        out_specs=(P(("spin",) + DOM, None, None), P("spin", None)),
         check_vma=False,
     )

time: 908 us -> 235 us (0.26)
  blocking collectives: 657 us -> 69.6 us
  starting transfers between devices: 117 us -> 30.7 us
    psum x1 -> x0, blocking collectives: 612 us -> none  [local(): gram_total = lax.psum(gram_part, 'dom')]
    all_to_all x1, starting transfers between devices: 75 us -> 6.94 us  [local(): lax.all_to_all(rotated, DOM, split_axis=0, concat_axis=1, tiled=True)]
    another operation x0 -> x3, other arithmetic: none -> 29.8 us
    all_to_all x1 -> x3, blocking collectives: 44.8 us -> 69.6 us  [the longest x1 44.8 us: local(): lax.all_to_all(orbitals, DOM, split_axis=1, concat_axis=0, tiled=True)]
    ppermute x4, starting transfers between devices: 33.9 us -> 9.89 us  [with_halo(): lax.ppermute(head, axis, [((i + 1) % count, i) for i in range(ends)])]
    sub x2 -> x0, other arithmetic: 21.5 us -> none  [local(): 2.0 * (apply_hamiltonian(current, potential_yx) - center * current)]
    ppermute x4, waiting for transfers between devices: 4.66 us -> 18.5 us  [with_halo(): lax.ppermute(head, axis, [((i + 1) % count, i) for i in range(ends)])]
    ppermute x4, waiting for transfers between devices: 39.3 us -> 26.2 us  [with_halo(): lax.ppermute(tail, axis, [(i, (i + 1) % count) for i in range(ends)])]
  transfers between devices with their start and end apart: 9 -> 9, of which waited for: 9 -> 9; matrix products, arithmetic and copies ran while one was open for 1% -> 2% of each run, Pallas kernels for 0% -> 0%
where the time goes in v1:
time: 235 us; the launch traced here: 234 us
  blocking collectives  69.6 us (30%)
  waiting for transfers between devices  66 us (28%)
  other arithmetic  46.7 us (20%)
  starting transfers between devices  30.7 us (13%)
  matrix products  11 us (5%)
  local copies, waits for them, and re-layouts  8.18 us (3%)
    all_to_all x1, blocking collectives, local(): lax.all_to_all(orbitals, DOM, split_axis=1, concat_axis=0, tiled=True)  44.8 us
    another operation x3, other arithmetic  29.8 us
    ppermute x4, waiting for transfers between devices, with_halo(): lax.ppermute(tail, axis, [(i, (i + 1) % count) for i in range(ends)])  26.2 us
    all_to_all x2, blocking collectives, sum_over(): lax.all_to_all(copies, axes, split_axis=0, concat_axis=0, tiled=True)  24.8 us
    all_to_all x1, waiting for transfers between devices, local(): lax.all_to_all(rotated, DOM, split_axis=0, concat_axis=1, tiled=True)  21.3 us
    ppermute x4, waiting for transfers between devices, with_halo(): lax.ppermute(head, axis, [((i + 1) % count, i) for i in range(ends)])  18.5 us
    ppermute x4, starting transfers between devices, with_halo(): lax.ppermute(tail, axis, [(i, (i + 1) % count) for i in range(ends)])  13.9 us
    ppermute x4, starting transfers between devices, with_halo(): lax.ppermute(head, axis, [((i + 1) % count, i) for i in range(ends)])  9.89 us
  transfers between devices with their start and end apart: 9, of which 9 were waited for; matrix products, arithmetic and copies ran while one was open for 2% of the time, Pallas kernels for 0%

profile of v1, /device:TPU:2, one launch (start us, length us, event | category | flops | bytes accessed | tf_op | source)
XLA Modules:
  0.0 234.4 jit_solution(17411910583227496483)
XLA Ops:
  0.6 2.8 %copy.41 = bf16[2,2048,128]{2,0,1:T(2,128)(2,1)S(1)} copy(bf16[2,2048,128]{2,1,0:T(8,128)(2,1)} %param.4) | data formatting | bytes 2097152 | tf_op args[0]
  3.5 44.8 %all_to_all.37 = bf16[2,2048,128]{2,0,1:T(2,128)(2,1)S(1)} all-to-all(bf16[2,2048,128]{2,0,1:T(2,128)(2,1)S(1)} %copy.41), channel_id=1, replica_groups=mesh['spin'=2,'x'=4,'z'=8,'y'=4] {'x','z','y'}, dimensions={1} | all-to-all | bytes 2097152 | tf_op jit(solution)/shard_map/all_to_all | solution.py:84
  48.3 0.1 copy.42
  48.4 0.2 copy.43
  48.6 0.2 fusion.307
  48.9 4.0 %collective-permute-start = (bf16[32,8,6,128]{3,2,1,0:T(8,128)(2,1)S(1)}, bf16[32,8,6,128]{3,2,1,0:T(8,128)(2,1)S(1)}, u32[]{:S(2)}, u32[]{:S(2)}) collective-permute-start(bf16[32,8,6,128]{3,2,1,0:T(8,128)(2,1)S(1)} %get-tuple-element.14), channel_id=1, source_target_pairs={{1,0},{2,1},{3,2},{4,3},{5,4},{6,5},{7,6},{8,7},{9,8},{10,9},{11,1... | collective-permute-start | bytes 1179656 | tf_op jit(solution)/shard_map/ppermute | solution.py:30
  52.9 1.9 collective-permute-start.1
  56.1 0.3 bitcast_convert_fusion
  56.4 5.2 %collective-permute-done = bf16[32,8,6,128]{3,2,1,0:T(8,128)(2,1)S(1)} collective-permute-done((bf16[32,8,6,128]{3,2,1,0:T(8,128)(2,1)S(1)}, bf16[32,8,6,128]{3,2,1,0:T(8,128)(2,1)S(1)}, u32[]{:S(2)}, u32[]{:S(2)}) %collective-permute-start) | collective-permute-done | bytes 393248 | tf_op jit(solution)/shard_map/ppermute | solution.py:30
  61.7 8.1 %collective-permute-done.1 = bf16[32,8,6,128]{3,2,1,0:T(8,128)(2,1)S(1)} collective-permute-done((bf16[32,8,6,128]{3,2,1,0:T(8,128)(2,1)S(1)}, bf16[32,8,6,128]{3,2,1,0:T(8,128)(2,1)S(1)}, u32[]{:S(2)}, u32[]{:S(2)}) %collective-permute-start.1) | collective-permute-done | bytes 393248 | tf_op jit(solution)/shard_map/ppermute | solution.py:29
  69.8 8.7 %fusion.302 = (bf16[32,8,16,128]{3,2,1,0:T(8,128)(2,1)S(1)}, f32[32,8,16,128]{3,2,1,0:T(8,128)S(1)}) fusion(f32[]{:T(128)} %bitcast.5, f32[32,8,16,128]{3,2,1,0:T(8,128)S(1)} %bitcast_convert_fusion, f32[]{:T(128)} %bitcast.4, f32[8,16,128]{2,1,0:T(8,128)S(1)} %copy.44, f32[32,8,6,128]{3,2,1,0:T(8,128)S(1)} %convert_element_type.58, ...), kind=kLoop, calls=%fused_computation.489 | loop fusion | flops 38797312 | bytes 6881288 | tf_op jit(solution)/shard_map/convert.8
  78.5 0.2 fusion.306
  78.8 1.9 collective-permute-start.2
  80.7 3.9 %collective-permute-start.3 = (bf16[32,8,6,128]{3,2,1,0:T(8,128)(2,1)S(1)}, bf16[32,8,6,128]{3,2,1,0:T(8,128)(2,1)S(1)}, u32[]{:S(2)}, u32[]{:S(2)}) collective-permute-start(bf16[32,8,6,128]{3,2,1,0:T(8,128)(2,1)S(1)} %get-tuple-element.13), channel_id=1, source_target_pairs={{0,1},{1,2},{2,3},{3,4},{4,5},{5,6},{6,7},{7,8},{8,9},{9,10},{10,1... | collective-permute-start | bytes 1179656 | tf_op jit(solution)/shard_map/ppermute | solution.py:29
  84.6 5.9 %collective-permute-done.2 = bf16[32,8,6,128]{3,2,1,0:T(8,128)(2,1)S(1)} collective-permute-done((bf16[32,8,6,128]{3,2,1,0:T(8,128)(2,1)S(1)}, bf16[32,8,6,128]{3,2,1,0:T(8,128)(2,1)S(1)}, u32[]{:S(2)}, u32[]{:S(2)}) %collective-permute-start.2) | collective-permute-done | bytes 393248 | tf_op jit(solution)/shard_map/ppermute | solution.py:30
  90.6 6.1 %collective-permute-done.3 = bf16[32,8,6,128]{3,2,1,0:T(8,128)(2,1)S(1)} collective-permute-done((bf16[32,8,6,128]{3,2,1,0:T(8,128)(2,1)S(1)}, bf16[32,8,6,128]{3,2,1,0:T(8,128)(2,1)S(1)}, u32[]{:S(2)}, u32[]{:S(2)}) %collective-permute-start.3) | collective-permute-done | bytes 393248 | tf_op jit(solution)/shard_map/ppermute | solution.py:29
  96.7 9.6 %fusion.300 = (bf16[32,8,16,128]{3,2,1,0:T(8,128)(2,1)S(1)}, f32[32,8,16,128]{3,2,1,0:T(8,128)}) fusion(f32[]{:T(128)} %bitcast.5, f32[32,8,16,128]{3,2,1,0:T(8,128)S(1)} %get-tuple-element.7, f32[]{:T(128)} %bitcast.4, f32[8,16,128]{2,1,0:T(8,128)S(1)} %copy.44, f32[32,8,6,128]{3,2,1,0:T(8,128)S(1)} %convert_element_type.60, ...), kind=kLoop, calls=%fused_computation.488 | loop fusion | flops 40370176 | bytes 7929864 | tf_op jit(solution)/shard_map/convert.6
  106.3 0.2 fusion.305
  106.6 2.1 collective-permute-start.4
  108.7 3.9 %collective-permute-start.5 = (bf16[32,8,6,128]{3,2,1,0:T(8,128)(2,1)S(1)}, bf16[32,8,6,128]{3,2,1,0:T(8,128)(2,1)S(1)}, u32[]{:S(2)}, u32[]{:S(2)}) collective-permute-start(bf16[32,8,6,128]{3,2,1,0:T(8,128)(2,1)S(1)} %get-tuple-element.11), channel_id=1, source_target_pairs={{0,1},{1,2},{2,3},{3,4},{4,5},{5,6},{6,7},{7,8},{8,9},{9,10},{10,1... | collective-permute-start | bytes 1179656 | tf_op jit(solution)/shard_map/ppermute | solution.py:29
  112.6 5.2 %collective-permute-done.4 = bf16[32,8,6,128]{3,2,1,0:T(8,128)(2,1)S(1)} collective-permute-done((bf16[32,8,6,128]{3,2,1,0:T(8,128)(2,1)S(1)}, bf16[32,8,6,128]{3,2,1,0:T(8,128)(2,1)S(1)}, u32[]{:S(2)}, u32[]{:S(2)}) %collective-permute-start.4) | collective-permute-done | bytes 393248 | tf_op jit(solution)/shard_map/ppermute | solution.py:30
  117.9 6.1 %collective-permute-done.5 = bf16[32,8,6,128]{3,2,1,0:T(8,128)(2,1)S(1)} collective-permute-done((bf16[32,8,6,128]{3,2,1,0:T(8,128)(2,1)S(1)}, bf16[32,8,6,128]{3,2,1,0:T(8,128)(2,1)S(1)}, u32[]{:S(2)}, u32[]{:S(2)}) %collective-permute-start.5) | collective-permute-done | bytes 393248 | tf_op jit(solution)/shard_map/ppermute | solution.py:29
  123.9 1.1 convert_element_type.62
  125.0 11.5 %fusion.298 = (bf16[32,8,16,128]{3,2,1,0:T(8,128)(2,1)}, f32[32,8,16,128]{3,2,1,0:T(8,128)S(1)}) fusion(f32[32,8,16,128]{3,2,1,0:T(8,128)S(1)} %get-tuple-element.7, f32[]{:T(128)} %bitcast.5, f32[32,8,16,128]{3,2,1,0:T(8,128)S(1)} %copy-done, f32[]{:T(128)} %bitcast.4, f32[8,16,128]{2,1,0:T(8,128)S(1)} %copy.44, ...), kind=kLoop, calls=%fused_computation.487 | loop fusion | flops 39845888 | bytes 8978440 | tf_op jit(solution)/shard_map/convert.4
  136.5 1.4 fusion.304
  137.8 1.9 collective-permute-start.6
  139.8 4.1 %collective-permute-start.7 = (bf16[32,8,6,128]{3,2,1,0:T(8,128)(2,1)S(1)}, bf16[32,8,6,128]{3,2,1,0:T(8,128)(2,1)S(1)}, u32[]{:S(2)}, u32[]{:S(2)}) collective-permute-start(bf16[32,8,6,128]{3,2,1,0:T(8,128)(2,1)S(1)} %get-tuple-element.9), channel_id=1, source_target_pairs={{0,1},{1,2},{2,3},{3,4},{4,5},{5,6},{6,7},{7,8},{8,9},{9,10},{10,1... | collective-permute-start | bytes 1179656 | tf_op jit(solution)/shard_map/ppermute | solution.py:29
  143.9 2.8 %fusion.281 = f32[32,32]{0,1:T(8,128)S(1)} fusion(f32[32,8,16,128]{3,2,1,0:T(8,128)S(1)} %get-tuple-element.3), kind=kOutput, calls=%fused_computation.466 | convolution fusion | flops 201326592 | bytes 2101248 | tf_op jit(solution)/shard_map/dot_general | solution.py:46
  146.7 2.2 collective-permute-done.6
  148.9 0.1 convert_element_type.63
  149.0 6.1 %collective-permute-done.7 = bf16[32,8,6,128]{3,2,1,0:T(8,128)(2,1)S(1)} collective-permute-done((bf16[32,8,6,128]{3,2,1,0:T(8,128)(2,1)S(1)}, bf16[32,8,6,128]{3,2,1,0:T(8,128)(2,1)S(1)}, u32[]{:S(2)}, u32[]{:S(2)}) %collective-permute-start.7) | collective-permute-done | bytes 393248 | tf_op jit(solution)/shard_map/ppermute | solution.py:29
  155.1 8.2 %fusion.10 = f32[32,8,16,128]{3,2,1,0:T(8,128)S(1)} fusion(f32[32,8,16,128]{3,2,1,0:T(8,128)S(1)} %get-tuple-element.3, f32[32,8,6,128]{3,2,1,0:T(8,128)S(1)} %convert_element_type.64, f32[32,8,6,128]{3,2,1,0:T(8,128)S(1)} %convert_element_type.63, f32[8,16,128]{2,1,0:T(8,128)S(1)} %copy.44), kind=kLoop, calls=%fused_computation.187 | loop fusion | flops 36700160 | bytes 5832704 | tf_op jit(solution)/shard_map/add | solution.py:72
  163.4 4.0 %fusion.284 = f32[32,32]{0,1:T(8,128)S(1)} fusion(f32[32,8,16,128]{3,2,1,0:T(8,128)S(1)} %fusion.10, f32[32,8,16,128]{3,2,1,0:T(8,128)S(1)} %get-tuple-element.3), kind=kOutput, calls=%fused_computation.467 | convolution fusion | flops 201326592 | bytes 4198400 | tf_op jit(solution)/shard_map/dot_general | solution.py:46
  167.5 0.1 copy.49
  167.7 10.3 %all_to_all.38 = f32[16,16,128]{2,1,0:T(8,128)S(1)} all-to-all(f32[16,16,128]{2,1,0:T(8,128)S(1)} %broadcast_in_dim.8), channel_id=1, replica_groups=mesh['spin'=2,'x'=4,'z'=8,'y'=4] {'x','y'}, dimensions={0} | all-to-all | bytes 262144 | tf_op jit(solution)/shard_map/all_to_all | solution.py:42
  178.1 14.4 %all_to_all.39 = f32[8,16,128]{2,1,0:T(8,128)S(1)} all-to-all(f32[8,16,128]{2,1,0:T(8,128)S(1)} %broadcast_in_dim.9), channel_id=1, replica_groups=mesh['spin'=2,'x'=4,'z'=8,'y'=4] {'z'}, dimensions={0} | all-to-all | bytes 131072 | tf_op jit(solution)/shard_map/all_to_all | solution.py:42
  192.7 2.9 %cholesky.17 = f32[32,32]{1,0:T(8,128)S(1)} custom-call(f32[32,32]{1,0:T(8,128)S(1)} %fusion.295), custom_call_target="Cholesky" | custom-call | tf_op jit(solution)/shard_map/jit(cholesky)/cholesky | solution.py:113
  195.6 0.6 compare_reduce_fusion
  196.3 0.7 fusion.289
  196.9 2.4 %custom-call.7 = f32[1,32,32]{1,2,0:T(8,128)S(1)} custom-call(f32[1,32,32]{2,1,0:T(8,128)S(1)} %fusion.289), custom_call_target="InvertDiagBlocksLowerTriangular" | custom-call | tf_op jit(solution)/shard_map/jit(_solve_triangular)/triangular_solve | solution.py:114
  199.4 0.2 fusion.293
  199.6 3.0 %convolution_convert_fusion = bf16[32,16384]{1,0:T(8,128)(2,1)S(1)} fusion(f32[32,32]{1,0:T(8,128)S(1)} %fusion.293, f32[4,8,128,128]{3,2,1,0:T(8,128)S(1)} %bitcast.46), kind=kOutput, calls=%fused_computation.96 | convolution fusion | flops 201850880 | bytes 3149824 | tf_op jit(solution)/shard_map/dot_general | solution.py:117
  202.6 1.3 reshape.44
  203.9 6.9 %all-to-all-start.3 = ((bf16[256,16,128]{2,1,0:T(8,128)(2,1)}), bf16[256,16,128]{2,1,0:T(8,128)(2,1)S(1)}, u32[]{:S(2)}, u32[]{:S(2)}) async-start(bf16[256,16,128]{2,1,0:T(8,128)(2,1)} %reshape.44), calls=%async_computation.3 | async-start | bytes 2097152 | tf_op jit(solution)/shard_map/all_to_all | solution.py:121
  211.0 0.1 fusion.291
  211.2 0.8 fusion.308
  211.9 21.3 %all-to-all-done.3 = bf16[256,16,128]{2,1,0:T(8,128)(2,1)S(1)} async-done(((bf16[256,16,128]{2,1,0:T(8,128)(2,1)}), bf16[256,16,128]{2,1,0:T(8,128)(2,1)S(1)}, u32[]{:S(2)}, u32[]{:S(2)}) %all-to-all-start.3) | async-done | bytes 1048608 | tf_op jit(solution)/shard_map/all_to_all | solution.py:121
  233.3 1.1 copy.51
  (24 shorter events, 1.0 us)
Async XLA Ops:
  48.4 7.7 %copy-start.1 = (f32[16,8,128]{2,1,0:T(8,128)S(1)}, f32[16,8,128]{2,1,0:T(8,128)}, u32[]{:S(2)}) copy-start(f32[16,8,128]{2,1,0:T(8,128)} %param.5) | copy-start | bytes 196612
  48.9 12.7 %collective-permute-start = (bf16[32,8,6,128]{3,2,1,0:T(8,128)(2,1)S(1)}, bf16[32,8,6,128]{3,2,1,0:T(8,128)(2,1)S(1)}, u32[]{:S(2)}, u32[]{:S(2)}) collective-permute-start(bf16[32,8,6,128]{3,2,1,0:T(8,128)(2,1)S(1)} %get-tuple-element.14), channel_id=1, source_target_pairs={{1,0},{2,1},{3,2},{4,3},{5,4},{6,5},{7,6},{8,7},{9,8},{10,9},{11,1... | collective-permute-start | bytes 1179656 | tf_op jit(solution)/shard_map/ppermute | solution.py:30
  52.9 16.9 %collective-permute-start.1 = (bf16[32,8,6,128]{3,2,1,0:T(8,128)(2,1)S(1)}, bf16[32,8,6,128]{3,2,1,0:T(8,128)(2,1)S(1)}, u32[]{:S(2)}, u32[]{:S(2)}) collective-permute-start(bf16[32,8,6,128]{3,2,1,0:T(8,128)(2,1)S(1)} %get-tuple-element.15), channel_id=1, source_target_pairs={{0,1},{1,2},{2,3},{3,4},{4,5},{5,6},{6,7},{7,8},{8,9},{9,10},{10,1... | collective-permute-start | bytes 1179656 | tf_op jit(solution)/shard_map/ppermute | solution.py:29
  78.8 11.7 %collective-permute-start.2 = (bf16[32,8,6,128]{3,2,1,0:T(8,128)(2,1)S(1)}, bf16[32,8,6,128]{3,2,1,0:T(8,128)(2,1)S(1)}, u32[]{:S(2)}, u32[]{:S(2)}) collective-permute-start(bf16[32,8,6,128]{3,2,1,0:T(8,128)(2,1)S(1)} %get-tuple-element.12), channel_id=1, source_target_pairs={{1,0},{2,1},{3,2},{4,3},{5,4},{6,5},{7,6},{8,7},{9,8},{10,9},{11,1... | collective-permute-start | bytes 1179656 | tf_op jit(solution)/shard_map/ppermute | solution.py:30
  80.7 15.9 %collective-permute-start.3 = (bf16[32,8,6,128]{3,2,1,0:T(8,128)(2,1)S(1)}, bf16[32,8,6,128]{3,2,1,0:T(8,128)(2,1)S(1)}, u32[]{:S(2)}, u32[]{:S(2)}) collective-permute-start(bf16[32,8,6,128]{3,2,1,0:T(8,128)(2,1)S(1)} %get-tuple-element.13), channel_id=1, source_target_pairs={{0,1},{1,2},{2,3},{3,4},{4,5},{5,6},{6,7},{7,8},{8,9},{9,10},{10,1... | collective-permute-start | bytes 1179656 | tf_op jit(solution)/shard_map/ppermute | solution.py:29
  106.6 18.4 %copy-start = (f32[32,8,16,128]{3,2,1,0:T(8,128)S(1)}, f32[32,8,16,128]{3,2,1,0:T(8,128)}, u32[]{:S(2)}) copy-start(f32[32,8,16,128]{3,2,1,0:T(8,128)} %get-tuple-element.5) | copy-start | bytes 6291460
  106.6 11.2 %collective-permute-start.4 = (bf16[32,8,6,128]{3,2,1,0:T(8,128)(2,1)S(1)}, bf16[32,8,6,128]{3,2,1,0:T(8,128)(2,1)S(1)}, u32[]{:S(2)}, u32[]{:S(2)}) collective-permute-start(bf16[32,8,6,128]{3,2,1,0:T(8,128)(2,1)S(1)} %get-tuple-element.10), channel_id=1, source_target_pairs={{1,0},{2,1},{3,2},{4,3},{5,4},{6,5},{7,6},{8,7},{9,8},{10,9},{11,1... | collective-permute-start | bytes 1179656 | tf_op jit(solution)/shard_map/ppermute | solution.py:30
  108.7 15.3 %collective-permute-start.5 = (bf16[32,8,6,128]{3,2,1,0:T(8,128)(2,1)S(1)}, bf16[32,8,6,128]{3,2,1,0:T(8,128)(2,1)S(1)}, u32[]{:S(2)}, u32[]{:S(2)}) collective-permute-start(bf16[32,8,6,128]{3,2,1,0:T(8,128)(2,1)S(1)} %get-tuple-element.11), channel_id=1, source_target_pairs={{0,1},{1,2},{2,3},{3,4},{4,5},{5,6},{6,7},{7,8},{8,9},{9,10},{10,1... | collective-permute-start | bytes 1179656 | tf_op jit(solution)/shard_map/ppermute | solution.py:29
  137.8 11.1 %collective-permute-start.6 = (bf16[32,8,6,128]{3,2,1,0:T(8,128)(2,1)S(1)}, bf16[32,8,6,128]{3,2,1,0:T(8,128)(2,1)S(1)}, u32[]{:S(2)}, u32[]{:S(2)}) collective-permute-start(bf16[32,8,6,128]{3,2,1,0:T(8,128)(2,1)S(1)} %get-tuple-element.8), channel_id=1, source_target_pairs={{1,0},{2,1},{3,2},{4,3},{5,4},{6,5},{7,6},{8,7},{9,8},{10,9},{11,1... | collective-permute-start | bytes 1179656 | tf_op jit(solution)/shard_map/ppermute | solution.py:30
  139.8 15.3 %collective-permute-start.7 = (bf16[32,8,6,128]{3,2,1,0:T(8,128)(2,1)S(1)}, bf16[32,8,6,128]{3,2,1,0:T(8,128)(2,1)S(1)}, u32[]{:S(2)}, u32[]{:S(2)}) collective-permute-start(bf16[32,8,6,128]{3,2,1,0:T(8,128)(2,1)S(1)} %get-tuple-element.9), channel_id=1, source_target_pairs={{0,1},{1,2},{2,3},{3,4},{4,5},{5,6},{6,7},{7,8},{8,9},{9,10},{10,1... | collective-permute-start | bytes 1179656 | tf_op jit(solution)/shard_map/ppermute | solution.py:29
  203.9 29.3 %all-to-all-start.3 = ((bf16[256,16,128]{2,1,0:T(8,128)(2,1)}), bf16[256,16,128]{2,1,0:T(8,128)(2,1)S(1)}, u32[]{:S(2)}, u32[]{:S(2)}) async-start(bf16[256,16,128]{2,1,0:T(8,128)(2,1)} %reshape.44), calls=%async_computation.3 | async-start | bytes 2097152 | tf_op jit(solution)/shard_map/all_to_all | solution.py:121

commit v2 on v1

v2 whole, which is shorter than its diff:
```python
import jax
import jax.numpy as jnp
import numpy as np
from jax import lax
from jax.experimental import pallas as pl
from jax.experimental.pallas import tpu as pltpu
from jax.sharding import Mesh, PartitionSpec as P

DOM = ("x", "z", "y")
BLOCKS = ("y", "z")

STENCIL = (
    -5369.0 / 1800.0,
    12.0 / 7.0,
    -15.0 / 56.0,
    10.0 / 189.0,
    -1.0 / 112.0,
    2.0 / 1925.0,
    -1.0 / 16632.0,
)
KINETIC = -2.0
SIDE = tuple(KINETIC * c for c in STENCIL[1:])
CENTRE = KINETIC * 3.0 * STENCIL[0]

NY = 8
NZ = 128
GROUP = 8
BANDS = 32
OWN = 64
HALO = 24
SPAN = OWN + 2 * HALO
SLAB = 16
AHEAD = 6
SENT = SLAB + AHEAD
ROWS = NY * GROUP
VMEM_LIMIT = 48 * 1024 * 1024


def split_bf16(value):
    high = value.astype(jnp.bfloat16)
    low = (value - high.astype(jnp.float32)).astype(jnp.bfloat16)
    return high, low


def z_matrix(sides):
    band = np.zeros((NZ, NZ), np.float64)
    for offset in range(1, 7):
        for cell in range(NZ - offset):
            band[cell + offset, cell] = SIDE[offset - 1]
            if sides == 2:
                band[cell, cell + offset] = SIDE[offset - 1]
    band = band.astype(np.float32)
    high = band.astype(jnp.bfloat16)
    low = (band - high.astype(np.float32)).astype(jnp.bfloat16)
    return high, low


def filter_kernel(
    scal, base, own, left, right, v_left, v_own, v_right, kz,
    out, own_f, left_f, right_f, u, s, y1, y2, y3,
):
    scale = scal[0]
    offset = scal[1]
    u[pl.ds(0, HALO * NY)] = (v_left[...] + offset) * scale
    u[pl.ds(HALO * NY, OWN * NY)] = (v_own[...] + offset) * scale
    u[pl.ds((HALO + OWN) * NY, HALO * NY)] = (v_right[...] + offset) * scale
    own_f[...] = own[...].astype(jnp.float32)
    left_f[...] = left[...].astype(jnp.float32)
    right_f[...] = right[...].astype(jnp.float32)

    def bring(source, planes, first):
        def step(x, carry):
            for y in range(NY):
                start = ((y // 2) * GROUP * 2 + y % 2) * planes + x
                s[first + x, pl.ds(y * GROUP, GROUP), :] = source[
                    pl.ds(start, GROUP, stride=2 * planes), :
                ]
            return carry

        lax.fori_loop(0, planes, step, 0, unroll=8)

    bring(left_f, HALO, 0)
    bring(own_f, OWN, HALO)
    bring(right_f, HALO, HALO + OWN)

    def level(source, source_first, before, before_first, target, first, last, start):
        def step(t, carry):
            i = first + 2 * t
            at = i - source_first
            block = source[pl.ds(at, 2)].reshape(2 * ROWS, NZ)
            if start:
                z = jnp.dot(
                    block.astype(jnp.bfloat16), kz[:NZ], preferred_element_type=jnp.float32
                )
            else:
                high, low = split_bf16(block)
                z = jnp.dot(
                    jnp.concatenate([high, low], axis=1), kz[...],
                    preferred_element_type=jnp.float32,
                )
            z = z[:, :NZ] + z[:, NZ:]
            for p in range(2):
                plane = base[0] + i + p
                inside = (plane >= 0) & (plane < base[1])
                factor = jnp.where(inside, scale, 0.0)
                cells = [block[p * ROWS + y * GROUP : p * ROWS + (y + 1) * GROUP] for y in range(NY)]
                for y in range(NY):
                    here = pl.ds(y * GROUP, GROUP)
                    total = z[p * ROWS + y * GROUP : p * ROWS + (y + 1) * GROUP]
                    for k in range(1, 7):
                        pair = source[at + p + k, here, :] + source[at + p - k, here, :]
                        if y + k < NY:
                            pair = pair + cells[y + k]
                        if y - k >= 0:
                            pair = pair + cells[y - k]
                        total = total + SIDE[k - 1] * pair
                    local = jnp.broadcast_to(u[pl.ds((i + p) * NY + y, 1), :], (GROUP, NZ))
                    value = factor * total + local * cells[y]
                    if start:
                        value = 0.5 * value
                    else:
                        value = value - before[i + p - before_first, here, :]
                    target[i + p - first, here, :] = value
            return carry

        lax.fori_loop(0, (last - first) // 2, step, 0)

    level(s, 0, None, 0, y1, 12, 106, True)
    level(y1, 12, s, 0, y2, 18, 100, False)
    level(y2, 18, y1, 12, y3, 24, 94, False)
    for dest in range(OWN // SLAB):
        out[dest] = y3[pl.ds(dest * SLAB, SENT)].astype(jnp.bfloat16)


def filtered_planes(scal, base, own, left, right, v_left, v_own, v_right):
    high, low = z_matrix(2)
    zero = np.zeros_like(high)
    kz = jnp.asarray(np.block([[high, low], [high, zero]]))
    smem = pl.BlockSpec(memory_space=pltpu.SMEM)
    vmem = pl.BlockSpec(memory_space=pltpu.VMEM)
    f32 = jnp.float32
    return pl.pallas_call(
        filter_kernel,
        out_shape=jax.ShapeDtypeStruct((OWN // SLAB, SENT, ROWS, NZ), jnp.bfloat16),
        in_specs=[smem, smem] + [vmem] * 7,
        out_specs=vmem,
        scratch_shapes=[
            pltpu.VMEM((ROWS * OWN, NZ), f32),
            pltpu.VMEM((ROWS * HALO, NZ), f32),
            pltpu.VMEM((ROWS * HALO, NZ), f32),
            pltpu.VMEM((SPAN * NY, NZ), f32),
            pltpu.VMEM((SPAN, ROWS, NZ), f32),
            pltpu.VMEM((94, ROWS, NZ), f32),
            pltpu.VMEM((82, ROWS, NZ), f32),
            pltpu.VMEM((70, ROWS, NZ), f32),
        ],
        compiler_params=pltpu.CompilerParams(vmem_limit_bytes=VMEM_LIMIT),
        name="filter_planes",
    )(scal, base, own, left, right, v_left, v_own, v_right, kz)


def sums_kernel(planes, v, kz, out, cells_f, total):
    def unpack(x, carry):
        for g in range(BANDS // GROUP):
            part = planes[g, x].astype(jnp.float32).reshape(NY, GROUP, NZ)
            cells_f[x, :, pl.ds(g * GROUP, GROUP), :] = part
        return carry

    lax.fori_loop(0, SENT, unpack, 0)
    total[...] = jnp.zeros_like(total)

    def step(x, carry):
        block = cells_f[x].reshape(NY * BANDS, NZ)
        block16 = block.astype(jnp.bfloat16)
        z = jnp.dot(block16, kz[...], preferred_element_type=jnp.float32)
        z = z[:, :NZ] + z[:, NZ:]
        cells = [block[y * BANDS : (y + 1) * BANDS] for y in range(NY)]
        cells16 = [block16[y * BANDS : (y + 1) * BANDS] for y in range(NY)]
        images = []
        for y in range(NY):
            image = z[y * BANDS : (y + 1) * BANDS]
            for k in range(1, 7):
                pair = cells_f[x + k, y]
                if y + k < NY:
                    pair = pair + cells[y + k]
                image = image + SIDE[k - 1] * pair
            local = jnp.broadcast_to(v[x, pl.ds(y, 1), :], (BANDS, NZ))
            image = image + (0.5 * (local + CENTRE)) * cells[y]
            images.append(image)
        add = total[...]
        for y in range(0, NY, 2):
            first = split_bf16(images[y])
            second = split_bf16(images[y + 1])
            lhs = jnp.concatenate([cells16[y], cells16[y + 1]], axis=1)
            rhs = jnp.concatenate(
                [
                    lhs,
                    jnp.concatenate([first[0], second[0]], axis=1),
                    jnp.concatenate([first[1], second[1]], axis=1),
                ],
                axis=0,
            )
            add = add + lax.dot_general(
                lhs, rhs, (((1,), (1,)), ((), ())), preferred_element_type=jnp.float32
            )
        total[...] = add
        return carry

    lax.fori_loop(0, SLAB, step, 0)
    sums = total[...]
    gram = sums[:, :BANDS]
    half = sums[:, BANDS : 2 * BANDS] + sums[:, 2 * BANDS :]
    both = jnp.concatenate([gram, half], axis=1)
    row = jnp.concatenate([both[:16], both[16:]], axis=1)
    for copy in range(out.shape[0]):
        out[copy] = row


def matrix_sums(planes, v, copies):
    kz = jnp.asarray(np.concatenate(z_matrix(1), axis=1))
    vmem = pl.BlockSpec(memory_space=pltpu.VMEM)
    f32 = jnp.float32
    return pl.pallas_call(
        sums_kernel,
        out_shape=jax.ShapeDtypeStruct((copies, 16, NZ), f32),
        in_specs=[vmem] * 3,
        out_specs=vmem,
        scratch_shapes=[
            pltpu.VMEM((SENT, NY, BANDS, NZ), f32),
            pltpu.VMEM((BANDS, 3 * BANDS), f32),
        ],
        compiler_params=pltpu.CompilerParams(vmem_limit_bytes=VMEM_LIMIT),
        name="matrix_sums",
    )(planes, v, kz)


def rotate_kernel(count, parts, planes, out, projected, turned):
    sums = jnp.sum(parts[...], axis=0) * (1.0 / count)
    gram = jnp.concatenate([sums[:, :32], sums[:, 64:96]], axis=0)
    half = jnp.concatenate([sums[:, 32:64], sums[:, 96:]], axis=0)
    ham = half + half.T
    rows = lax.broadcasted_iota(jnp.int32, (BANDS, BANDS), 0)
    columns = lax.broadcasted_iota(jnp.int32, (BANDS, BANDS), 1)
    unit = jnp.where(rows == columns, 1.0, 0.0).astype(jnp.float32)
    work = jnp.concatenate([gram, unit], axis=1)
    index = lax.broadcasted_iota(jnp.int32, (BANDS, 1), 0)
    for k in range(BANDS):
        pivot = work[k : k + 1, k : k + 1]
        row = work[k : k + 1] / jnp.sqrt(pivot)
        lower = jnp.where(index > k, work[:, k : k + 1] / jnp.sqrt(pivot), 0.0)
        work = jnp.where(index == k, row, work - lower * row)
    inverse = work[:, BANDS:]
    high = lax.Precision.HIGHEST
    left = jnp.dot(inverse, ham, precision=high, preferred_element_type=jnp.float32)
    projected[...] = lax.dot_general(
        left, inverse, (((1,), (1,)), ((), ())), precision=high,
        preferred_element_type=jnp.float32,
    )
    both = jnp.concatenate(split_bf16(inverse), axis=1)

    def turn(x, carry):
        parts32 = [planes[g, x].astype(jnp.float32) for g in range(BANDS // GROUP)]
        wide = []
        for y in range(NY):
            wide.append(
                jnp.concatenate([p[y * GROUP : (y + 1) * GROUP] for p in parts32], axis=0)
            )
        data = jnp.concatenate(wide, axis=1).astype(jnp.bfloat16)
        data = jnp.concatenate([data, data], axis=0)
        result = jnp.dot(both, data, preferred_element_type=jnp.float32)
        for y in range(NY):
            start = pl.multiple_of((x * NY + y) * BANDS, BANDS)
            turned[pl.ds(start, BANDS), :] = result[:, y * NZ : (y + 1) * NZ]
        return carry

    lax.fori_loop(0, SLAB, turn, 0)

    def give(b, carry):
        for pair in range(NY // 2):
            for g in range(BANDS // GROUP):
                for odd in range(2):
                    start = (2 * pair + odd) * BANDS + g * GROUP + b
                    value = turned[pl.ds(start, SLAB, stride=NY * BANDS), :]
                    out[(pair * GROUP + b) * (BANDS // GROUP) + g, odd] = value.astype(jnp.bfloat16)
        return carry

    lax.fori_loop(0, GROUP, give, 0)


def rotated_planes(parts, planes, count):
    vmem = pl.BlockSpec(memory_space=pltpu.VMEM)

    def kernel(*refs):
        rotate_kernel(count, *refs)

    return pl.pallas_call(
        kernel,
        out_shape=(
            jax.ShapeDtypeStruct((128, 2, SLAB, NZ), jnp.bfloat16),
            jax.ShapeDtypeStruct((BANDS, BANDS), jnp.float32),
        ),
        in_specs=[vmem] * 2,
        out_specs=(vmem, vmem),
        scratch_shapes=[pltpu.VMEM((SLAB * NY * BANDS, NZ), jnp.float32)],
        compiler_params=pltpu.CompilerParams(vmem_limit_bytes=VMEM_LIMIT),
        name="rotate_planes",
    )(parts, planes)


def local(orbitals, potential, cutoff, ceiling):
    x_cells = orbitals.shape[1]
    block_count = x_cells // OWN
    center = 0.5 * (ceiling[0] + cutoff[0])
    half_width = 0.5 * (ceiling[0] - cutoff[0])
    scal = jnp.stack([2.0 / half_width, CENTRE - center])
    block_index = lax.axis_index(BLOCKS)
    base = jnp.stack([block_index * OWN - HALO, jnp.int32(x_cells)])
    place = [z * 4 + y for y in range(4) for z in range(8)]
    up = [(place[i], place[i + 1]) for i in range(block_count - 1)]
    down = [(b, a) for a, b in up]

    swap = [(a * 4 + b, b * 4 + a) for a in range(4) for b in range(4)]
    v_slab = lax.ppermute(potential, ("x", "y"), swap)
    v_own = lax.all_gather(v_slab, "x", tiled=True)
    v_left = lax.ppermute(v_own[OWN - HALO :], ("z", "y"), up)
    v_right = lax.ppermute(v_own[:HALO], ("z", "y"), down)

    chunks = orbitals.reshape(2, block_count, OWN, NZ).swapaxes(0, 1)
    own = lax.all_to_all(chunks, BLOCKS, split_axis=0, concat_axis=0, tiled=True)
    left = lax.ppermute(own[:, :, OWN - HALO :].reshape(ROWS * HALO, NZ), ("z", "y"), up)
    right = lax.ppermute(own[:, :, :HALO].reshape(ROWS * HALO, NZ), ("z", "y"), down)
    filtered = filtered_planes(
        scal,
        base,
        own.reshape(ROWS * OWN, NZ),
        left,
        right,
        v_left.reshape(HALO * NY, NZ),
        v_own.reshape(OWN * NY, NZ),
        v_right.reshape(HALO * NY, NZ),
    )
    planes = lax.all_to_all(filtered, "x", split_axis=0, concat_axis=0, tiled=True)
    sums = matrix_sums(planes, v_slab, 16)
    sums = lax.all_to_all(sums, ("x", "y"), split_axis=0, concat_axis=0, tiled=True)
    sums = jnp.broadcast_to(jnp.sum(sums, axis=0)[None], (8, 16, NZ))
    sums = lax.all_to_all(sums, "z", split_axis=0, concat_axis=0, tiled=True)
    rotated, projected = rotated_planes(sums, planes, x_cells * NY * NZ)
    returned = lax.all_to_all(rotated, ("y", "z", "x"), split_axis=0, concat_axis=0, tiled=True)
    returned = returned.swapaxes(0, 1).reshape(2, x_cells, NZ)
    return (returned, projected)


def solution(mesh):
    mesh = Mesh(mesh.devices.reshape(2, 4, 8, 4), ("spin",) + DOM)
    return jax.shard_map(
        local,
        mesh=mesh,
        in_specs=(
            P(("spin",) + DOM, None, None),
            P(("spin",) + DOM, None, None),
            P("spin"),
            P("spin"),
        ),
        out_specs=(P(("spin",) + DOM, None, None), P("spin", None)),
        check_vma=False,
    )
```

time: 235 us -> 182 us (0.77)
  other arithmetic: 46.7 us -> 0.17 us
  waiting for transfers between devices: 66 us -> 25.5 us
  Pallas kernels: 0 us -> 39.8 us
  blocking collectives: 69.6 us -> 83.1 us
  matrix products: 11 us -> 0 us
  local copies, waits for them, and re-layouts: 8.18 us -> 3.56 us
  starting transfers between devices: 30.7 us -> 26.8 us
    ppermute x8 -> x5, waiting for transfers between devices: 44.7 us -> 2.12 us  [the longest x1 1.54 us: local(): v_left = lax.ppermute(v_own[OWN - HALO:], ('z', 'y'), up)]
    pallas_call x0 -> x3, Pallas kernels: none -> 39.8 us  [the longest x1 26 us: filtered_planes(): pl.pallas_call(filter_kernel, out_shape=jax.ShapeDtypeStruct((OWN // SLAB...]
    another operation x8 -> x2, other arithmetic: 36.5 us -> 0.15 us  [the longest x1 0.08 us: local(): base = jnp.stack([block_index * OWN - HALO, jnp.int32(x_cells)])]
    all_gather x0 -> x1, blocking collectives: none -> 12.3 us  [local(): v_own = lax.all_gather(v_slab, 'x', tiled=True)]
    dot_general x5 -> x0, matrix products: 10.8 us -> none  [the longest x2 6.87 us: inner_products(): jnp.dot(left, right.T, precision=lax.Precision.HIGHEST, preferred_element...]
    ppermute x8 -> x5, starting transfers between devices: 23.8 us -> 15.2 us  [the longest x1 5.18 us: local(): v_left = lax.ppermute(v_own[OWN - HALO:], ('z', 'y'), up)]
    add x1 -> x0, other arithmetic: 8.24 us -> none  [stencil_apply(): return KINETIC * laplace + potential_yx * field]
    all_to_all x1, starting transfers between devices: 6.94 us -> 11.6 us  [local(): lax.all_to_all(chunks, BLOCKS, split_axis=0, concat_axis=0, tiled=True)]
  transfers between devices with their start and end apart: 9 -> 6, of which waited for: 9 -> 3; matrix products, arithmetic and copies ran while one was open for 2% -> 0% of each run, Pallas kernels for 0% -> 0%
where the time goes in v2:
time: 182 us; the launch traced here: 181 us
  blocking collectives  83.1 us (46%)
  Pallas kernels  39.8 us (22%)
  starting transfers between devices  26.8 us (15%)
  waiting for transfers between devices  25.5 us (14%)
  local copies, waits for them, and re-layouts  3.56 us (2%)
  between operations  2.12 us (1%)
    all_to_all x1, blocking collectives, local(): lax.all_to_all(rotated, ('y', 'z', 'x'), split_axis=0, concat_axis=0, til...  26.9 us
    pallas_call x1, Pallas kernels, filtered_planes(): pl.pallas_call(filter_kernel, out_shape=jax.ShapeDtypeStruct((OWN // SLAB...  26 us
    all_to_all x1, waiting for transfers between devices, local(): lax.all_to_all(chunks, BLOCKS, split_axis=0, concat_axis=0, tiled=True)  23.4 us
    all_to_all x1, blocking collectives, local(): lax.all_to_all(sums, ('x', 'y'), split_axis=0, concat_axis=0, tiled=True)  16.4 us
    all_to_all x1, blocking collectives, local(): lax.all_to_all(filtered, 'x', split_axis=0, concat_axis=0, tiled=True)  16 us
    all_gather x1, blocking collectives, local(): v_own = lax.all_gather(v_slab, 'x', tiled=True)  12.3 us
    all_to_all x1, starting transfers between devices, local(): lax.all_to_all(chunks, BLOCKS, split_axis=0, concat_axis=0, tiled=True)  11.6 us
    all_to_all x1, blocking collectives, local(): sums = lax.all_to_all(sums, 'z', split_axis=0, concat_axis=0, tiled=True)  11.5 us
  transfers between devices with their start and end apart: 6, of which 3 were waited for; matrix products, arithmetic and copies ran while one was open for 0% of the time, Pallas kernels for 0%

profile of v2, /device:TPU:2, one launch (start us, length us, event | category | flops | bytes accessed | tf_op | source)
XLA Modules:
  0.0 181.0 jit_solution(4978374269760060950)
XLA Ops:
  0.6 2.3 %copy.14 = bf16[2,32,64,128]{3,2,0,1:T(8,128)(2,1)} copy(bf16[2,32,64,128]{3,2,1,0:T(8,128)(2,1)} %bitcast.18) | data formatting | bytes 2097152 | tf_op jit(solution)/shard_map/reshape | solution.py:328
  2.9 0.0 copy-start.2
  2.9 11.6 %all-to-all-start = ((bf16[32,2,64,128]{3,2,1,0:T(8,128)(2,1)}), bf16[32,2,64,128]{3,2,1,0:T(8,128)(2,1)S(1)}, u32[]{:S(2)}, u32[]{:S(2)}) async-start(bf16[32,2,64,128]{3,2,1,0:T(8,128)(2,1)} %bitcast.12), calls=%async_computation | async-start | bytes 2097152 | tf_op jit(solution)/shard_map/all_to_all | solution.py:329
  14.5 0.0 copy-done.2
  14.6 0.0 copy-start
  14.6 3.8 %collective-permute-start.2 = (f32[16,8,128]{2,1,0:T(8,128)S(1)}, f32[16,8,128]{2,1,0:T(8,128)S(1)}, u32[]{:S(2)}, u32[]{:S(2)}) collective-permute-start(f32[16,8,128]{2,1,0:T(8,128)S(1)} %copy-done.2), channel_id=1, source_target_pairs={{0,0},{1,32},{2,64},{3,96},{32,1},{33,33},{34,65},{35,97},{64,2},{... | collective-permute-start | bytes 196616 | tf_op jit(solution)/shard_map/ppermute | solution.py:323
  19.7 0.1 pad_maximum_fusion.scal
  19.8 23.4 %all-to-all-done = bf16[32,2,64,128]{3,2,1,0:T(8,128)(2,1)S(1)} async-done(((bf16[32,2,64,128]{3,2,1,0:T(8,128)(2,1)}), bf16[32,2,64,128]{3,2,1,0:T(8,128)(2,1)S(1)}, u32[]{:S(2)}, u32[]{:S(2)}) %all-to-all-start) | async-done | bytes 1048608 | tf_op jit(solution)/shard_map/all_to_all | solution.py:329
  43.2 0.1 fusion
  43.3 3.6 %collective-permute-start = (bf16[1536,128]{1,0:T(8,128)(2,1)S(1)}, bf16[1536,128]{1,0:T(8,128)(2,1)S(1)}, u32[]{:S(2)}, u32[]{:S(2)}) collective-permute-start(bf16[1536,128]{1,0:T(8,128)(2,1)S(1)} %bitcast.21), channel_id=1, source_target_pairs={{0,4},{4,8},{8,12},{12,16},{16,20},{20,24},{24,28},{28,1},{1,5},{5... | collective-permute-start | bytes 1179656 | tf_op jit(solution)/shard_map/ppermute | solution.py:330
  46.9 1.3 collective-permute-start.1
  48.2 0.0 collective-permute-done.2.v
  48.2 12.3 %all_gather.3 = f32[64,8,128]{2,1,0:T(8,128)S(1)} all-gather(f32[16,8,128]{2,1,0:T(8,128)S(1)} %collective-permute-done.2.v), channel_id=1, replica_groups=mesh['spin'=2,'x'=4,'z'=8,'y'=4] {'x'}, dimensions={0}, use_global_device_ids=true | all-gather | bytes 327680 | tf_op jit(solution)/shard_map/all_gather | solution.py:324
  60.5 1.3 collective-permute-start.4
  61.8 5.2 %collective-permute-start.3 = (f32[24,8,128]{2,1,0:T(8,128)S(1)}, f32[24,8,128]{2,1,0:T(8,128)S(1)}, u32[]{:S(2)}, u32[]{:S(2)}) collective-permute-start(f32[24,8,128]{2,1,0:T(8,128)S(1)} %get-tuple-element.9), channel_id=1, source_target_pairs={{0,4},{4,8},{8,12},{12,16},{16,20},{20,24},{24,28},{28,1},{1,5},{5... | collective-permute-start | bytes 294920 | tf_op jit(solution)/shard_map/ppermute | solution.py:325
  67.0 0.1 pad_add_fusion.base
  67.1 0.6 collective-permute-done.4
  67.7 1.5 collective-permute-done.3
  69.2 0.0 collective-permute-done.left
  69.2 0.0 collective-permute-done.1.right
  69.2 0.0 copy-done
  69.2 26.0 %filter_planes.1 = bf16[4,22,64,128]{3,2,1,0:T(8,128)(2,1)S(1)} custom-call(f32[2]{0:T(128)S(1)} %pad_maximum_fusion.scal, s32[2]{0:T(128)S(1)} %pad_add_fusion.base, bf16[4096,128]{1,0:T(8,128)(2,1)S(1)} %bitcast.13, bf16[1536,128]{1,0:T(8,128)(2,1)S(1)} %collective-permute-done.left, bf16[1536,128]{1,0:T(8,128)(2,1)S(1)} %collective-permute-done.1.right, ...), custom_call_target="tpu_custom_call" | custom-call | tf_op jit(solution)/shard_map/filter_planes/pallas_call | solution.py:142
  95.2 0.0 copy-start.1
  95.2 16.0 %all_to_all.25.planes.refs_1_ = bf16[4,22,64,128]{3,2,1,0:T(8,128)(2,1)S(1)} all-to-all(bf16[4,22,64,128]{3,2,1,0:T(8,128)(2,1)S(1)} %filter_planes.1), channel_id=1, replica_groups=mesh['spin'=2,'x'=4,'z'=8,'y'=4] {'x'}, dimensions={0} | all-to-all | bytes 2883584 | tf_op jit(solution)/shard_map/all_to_all | solution.py:342
  111.2 0.0 copy-done.1
  111.2 6.3 %matrix_sums.1 = f32[16,16,128]{2,1,0:T(8,128)S(1)} custom-call(bf16[4,22,64,128]{3,2,1,0:T(8,128)(2,1)S(1)} %all_to_all.25.planes.refs_1_, f32[16,8,128]{2,1,0:T(8,128)S(1)} %collective-permute-done.2.v, bf16[128,256]{1,0:T(8,128)(2,1)S(1)} %copy-done.1), custom_call_target="tpu_custom_call" | custom-call | tf_op jit(solution)/shard_map/matrix_sums/pallas_call | solution.py:223
  117.5 16.4 %all_to_all.26 = f32[16,16,128]{2,1,0:T(8,128)S(1)} all-to-all(f32[16,16,128]{2,1,0:T(8,128)S(1)} %matrix_sums.1), channel_id=1, replica_groups=mesh['spin'=2,'x'=4,'z'=8,'y'=4] {'x','y'}, dimensions={0} | all-to-all | bytes 262144 | tf_op jit(solution)/shard_map/all_to_all | solution.py:344
  133.9 11.5 %all_to_all.27.refs_0_ = f32[8,16,128]{2,1,0:T(8,128)S(1)} all-to-all(f32[8,16,128]{2,1,0:T(8,128)S(1)} %broadcast_in_dim.2), channel_id=1, replica_groups=mesh['spin'=2,'x'=4,'z'=8,'y'=4] {'z'}, dimensions={0} | all-to-all | bytes 131072 | tf_op jit(solution)/shard_map/all_to_all | solution.py:346
  145.4 7.5 %rotate_planes.1 = (bf16[128,2,16,128]{3,2,1,0:T(8,128)(2,1)S(1)}, f32[32,32]{1,0:T(8,128)}) custom-call(f32[8,16,128]{2,1,0:T(8,128)S(1)} %all_to_all.27.refs_0_, bf16[4,22,64,128]{3,2,1,0:T(8,128)(2,1)S(1)} %all_to_all.25.planes.refs_1_), custom_call_target="tpu_custom_call" | custom-call | tf_op jit(solution)/shard_map/rotate_planes/pallas_call | solution.py:296
  153.0 26.9 %all_to_all.28 = bf16[128,2,16,128]{3,2,1,0:T(8,128)(2,1)S(1)} all-to-all(bf16[128,2,16,128]{3,2,1,0:T(8,128)(2,1)S(1)} %get-tuple-element.4), channel_id=1, replica_groups=mesh['spin'=2,'x'=4,'z'=8,'y'=4] {'y','z','x'}, dimensions={0} | all-to-all | bytes 2097152 | tf_op jit(solution)/shard_map/all_to_all | solution.py:348
  179.8 1.1 copy.12
  (3 shorter events, 0.0 us)
Async XLA Ops:
  2.9 11.6 %copy-start.2 = (f32[16,8,128]{2,1,0:T(8,128)S(1)}, f32[16,8,128]{2,1,0:T(8,128)}, u32[]{:S(2)}) copy-start(f32[16,8,128]{2,1,0:T(8,128)} %param.7) | copy-start | bytes 196612
  2.9 40.3 %all-to-all-start = ((bf16[32,2,64,128]{3,2,1,0:T(8,128)(2,1)}), bf16[32,2,64,128]{3,2,1,0:T(8,128)(2,1)S(1)}, u32[]{:S(2)}, u32[]{:S(2)}) async-start(bf16[32,2,64,128]{3,2,1,0:T(8,128)(2,1)} %bitcast.12), calls=%async_computation | async-start | bytes 2097152 | tf_op jit(solution)/shard_map/all_to_all | solution.py:329
  14.6 54.7 %copy-start = (bf16[256,256]{1,0:T(8,128)(2,1)S(1)}, bf16[256,256]{1,0:T(8,128)(2,1)}, u32[]{:S(2)}) copy-start(bf16[256,256]{1,0:T(8,128)(2,1)} %constant.34.clone.kz) | copy-start | bytes 393220
  14.6 33.6 %collective-permute-start.2 = (f32[16,8,128]{2,1,0:T(8,128)S(1)}, f32[16,8,128]{2,1,0:T(8,128)S(1)}, u32[]{:S(2)}, u32[]{:S(2)}) collective-permute-start(f32[16,8,128]{2,1,0:T(8,128)S(1)} %copy-done.2), channel_id=1, source_target_pairs={{0,0},{1,32},{2,64},{3,96},{32,1},{33,33},{34,65},{35,97},{64,2},{... | collective-permute-start | bytes 196616 | tf_op jit(solution)/shard_map/ppermute | solution.py:323
  43.3 25.9 %collective-permute-start = (bf16[1536,128]{1,0:T(8,128)(2,1)S(1)}, bf16[1536,128]{1,0:T(8,128)(2,1)S(1)}, u32[]{:S(2)}, u32[]{:S(2)}) collective-permute-start(bf16[1536,128]{1,0:T(8,128)(2,1)S(1)} %bitcast.21), channel_id=1, source_target_pairs={{0,4},{4,8},{8,12},{12,16},{16,20},{20,24},{24,28},{28,1},{1,5},{5... | collective-permute-start | bytes 1179656 | tf_op jit(solution)/shard_map/ppermute | solution.py:330
  46.9 22.3 %collective-permute-start.1 = (bf16[1536,128]{1,0:T(8,128)(2,1)S(1)}, bf16[1536,128]{1,0:T(8,128)(2,1)S(1)}, u32[]{:S(2)}, u32[]{:S(2)}) collective-permute-start(bf16[1536,128]{1,0:T(8,128)(2,1)S(1)} %bitcast.20), channel_id=1, source_target_pairs={{4,0},{8,4},{12,8},{16,12},{20,16},{24,20},{28,24},{1,28},{5,1},{9... | collective-permute-start | bytes 1179656 | tf_op jit(solution)/shard_map/ppermute | solution.py:331
  60.5 7.1 %collective-permute-start.4 = (f32[24,8,128]{2,1,0:T(8,128)S(1)}, f32[24,8,128]{2,1,0:T(8,128)S(1)}, u32[]{:S(2)}, u32[]{:S(2)}) collective-permute-start(f32[24,8,128]{2,1,0:T(8,128)S(1)} %get-tuple-element.8), channel_id=1, source_target_pairs={{4,0},{8,4},{12,8},{16,12},{20,16},{24,20},{28,24},{1,28},{5,1},{9... | collective-permute-start | bytes 294920 | tf_op jit(solution)/shard_map/ppermute | solution.py:326
  61.8 7.4 %collective-permute-start.3 = (f32[24,8,128]{2,1,0:T(8,128)S(1)}, f32[24,8,128]{2,1,0:T(8,128)S(1)}, u32[]{:S(2)}, u32[]{:S(2)}) collective-permute-start(f32[24,8,128]{2,1,0:T(8,128)S(1)} %get-tuple-element.9), channel_id=1, source_target_pairs={{0,4},{4,8},{8,12},{12,16},{16,20},{20,24},{24,28},{28,1},{1,5},{5... | collective-permute-start | bytes 294920 | tf_op jit(solution)/shard_map/ppermute | solution.py:325
  95.2 16.0 %copy-start.1 = (bf16[128,256]{1,0:T(8,128)(2,1)S(1)}, bf16[128,256]{1,0:T(8,128)(2,1)}, u32[]{:S(2)}) copy-start(bf16[128,256]{1,0:T(8,128)(2,1)} %constant.35.clone.kz) | copy-start | bytes 196612

commit v3 on v2

v3 whole, which is shorter than its diff:
```python
import jax
import jax.numpy as jnp
import numpy as np
from jax import lax
from jax.experimental import pallas as pl
from jax.experimental.pallas import tpu as pltpu
from jax.sharding import Mesh, PartitionSpec as P

DOM = ("x", "z", "y")
BLOCKS = ("y", "z")

STENCIL = (
    -5369.0 / 1800.0,
    12.0 / 7.0,
    -15.0 / 56.0,
    10.0 / 189.0,
    -1.0 / 112.0,
    2.0 / 1925.0,
    -1.0 / 16632.0,
)
KINETIC = -2.0
SIDE = tuple(KINETIC * c for c in STENCIL[1:])
CENTRE = KINETIC * 3.0 * STENCIL[0]

NY = 8
NZ = 128
GROUP = 8
BANDS = 32
OWN = 64
HALO = 24
SPAN = OWN + 2 * HALO
SLAB = 16
AHEAD = 6
SENT = SLAB + AHEAD
ROWS = NY * GROUP
EDGE = 12
PLANES = 8
VMEM_LIMIT = 48 * 1024 * 1024


def split_bf16(value):
    high = value.astype(jnp.bfloat16)
    low = (value - high.astype(jnp.float32)).astype(jnp.bfloat16)
    return high, low


def z_matrix(sides):
    band = np.zeros((NZ, NZ), np.float64)
    for offset in range(1, 7):
        for cell in range(NZ - offset):
            band[cell + offset, cell] = SIDE[offset - 1]
            if sides == 2:
                band[cell, cell + offset] = SIDE[offset - 1]
    band = band.astype(np.float32)
    high = band.astype(jnp.bfloat16)
    low = (band - high.astype(np.float32)).astype(jnp.bfloat16)
    return high, low


def level(
    kz, u, scale, base, source, source_first, before, before_first,
    target, target_first, first, last, count, start=False,
):
    def step(t, carry):
        i = first + count * t
        at = i - source_first
        block = source[pl.ds(at, count)].reshape(count * ROWS, NZ)
        if start:
            z = jnp.dot(block.astype(jnp.bfloat16), kz[:NZ], preferred_element_type=jnp.float32)
        else:
            z = jnp.dot(
                jnp.concatenate(split_bf16(block), axis=1), kz[...],
                preferred_element_type=jnp.float32,
            )
        for p in range(count):
            factor = scale
            if base is not None:
                plane = base[0] + i + p
                factor = jnp.where((plane >= 0) & (plane < base[1]), scale, 0.0)
            at_y = [slice(p * ROWS + y * GROUP, p * ROWS + (y + 1) * GROUP) for y in range(NY)]
            for y in range(NY):
                here = pl.ds(y * GROUP, GROUP)
                total = None
                for k in range(1, 7):
                    pair = source[at + p + k, here, :] + source[at + p - k, here, :]
                    if y + k < NY:
                        pair = pair + block[at_y[y + k]]
                    if y - k >= 0:
                        pair = pair + block[at_y[y - k]]
                    pair = SIDE[k - 1] * pair
                    total = pair if total is None else total + pair
                total = total + (z[at_y[y], :NZ] + z[at_y[y], NZ:])
                local = jnp.broadcast_to(u[pl.ds((i + p) * NY + y, 1), :], (GROUP, NZ))
                value = factor * total + local * block[at_y[y]]
                if start:
                    value = 0.5 * value
                else:
                    value = value - before[i + p - before_first, here, :]
                target[i + p - target_first, here, :] = value
        return carry

    lax.fori_loop(0, (last - first) // count, step, 0)


def bring(source, planes, target, first):
    def step(x, carry):
        for y in range(NY):
            start = ((y // 2) * GROUP * 2 + y % 2) * planes + x
            target[first + x, pl.ds(y * GROUP, GROUP), :] = source[
                pl.ds(start, GROUP, stride=2 * planes), :
            ]
        return carry

    lax.fori_loop(0, planes, step, 0, unroll=8)


def inner_kernel(scal, own, v_own, kz, s_edge, y1_edge, y2_edge, y3_inner, own_f, u, s, y1, y2, y3):
    scale = scal[0]
    u[pl.ds(HALO * NY, OWN * NY)] = (v_own[...] + scal[1]) * scale
    own_f[...] = own[...].astype(jnp.float32)
    bring(own_f, OWN, s, 0)
    level(kz, u, scale, None, s, 24, None, 0, y1, 30, 30, 82, 13, start=True)
    level(kz, u, scale, None, y1, 30, s, 24, y2, 36, 36, 76, 10)
    level(kz, u, scale, None, y2, 36, y1, 30, y3, 42, 42, 70, 14)
    for ref, edge in ((s, s_edge), (y1, y1_edge), (y2, y2_edge)):
        edge[0] = ref[pl.ds(0, EDGE)]
        edge[1] = ref[pl.ds(ref.shape[0] - EDGE, EDGE)]
    y3_inner[...] = y3[...].astype(jnp.bfloat16)


def outer_kernel(
    scal, base, left, right, v_own, s_edge, y1_edge, y2_edge, y3_inner, kz,
    out, side_f, u, s, y1, y2, y3,
):
    scale = scal[0]
    v_rows = HALO * NY
    u[pl.ds(v_rows, OWN * NY)] = (v_own[...] + scal[1]) * scale
    y3[pl.ds(18, 28)] = y3_inner[...].astype(jnp.float32)
    for side, halo in ((0, left), (1, right)):
        field_rows = ROWS * HALO
        side_f[...] = halo[...].astype(jnp.float32)
        v = side_f[pl.ds(field_rows, v_rows)] + side_f[pl.ds(field_rows + v_rows, v_rows)]
        u[pl.ds(side * (HALO + OWN) * NY, v_rows)] = (v + scal[1]) * scale
        halo_at, edge_at = ((0, HALO), (EDGE, 0))[side]
        bring(side_f, HALO, s, halo_at)
        s[pl.ds(edge_at, EDGE)] = s_edge[side]
        y1_at, y2_at = ((18, 18), (0, 0))[side]
        y1[pl.ds(y1_at, EDGE)] = y1_edge[side]
        y2[pl.ds(y2_at, EDGE)] = y2_edge[side]
        if side == 0:
            level(kz, u, scale, base, s, 0, None, 0, y1, 12, 12, 30, 9, start=True)
            level(kz, u, scale, base, y1, 12, s, 0, y2, 18, 18, 36, 9)
            level(kz, u, scale, base, y2, 18, y1, 12, y3, 24, 24, 42, 9)
        else:
            level(kz, u, scale, base, s, 76, None, 0, y1, 70, 82, 106, 12, start=True)
            level(kz, u, scale, base, y1, 70, s, 76, y2, 64, 76, 100, 12)
            level(kz, u, scale, base, y2, 64, y1, 70, y3, 24, 70, 94, 12)
    for dest in range(OWN // SLAB):
        out[dest] = y3[pl.ds(dest * SLAB, SENT)].astype(jnp.bfloat16)


def z_both():
    high, low = z_matrix(2)
    return jnp.asarray(np.block([[high, low], [high, np.zeros_like(high)]]))


def inner_planes(scal, own, v_own):
    smem = pl.BlockSpec(memory_space=pltpu.SMEM)
    vmem = pl.BlockSpec(memory_space=pltpu.VMEM)
    f32 = jnp.float32
    edge = jax.ShapeDtypeStruct((2, EDGE, ROWS, NZ), f32)
    return pl.pallas_call(
        inner_kernel,
        out_shape=(edge, edge, edge, jax.ShapeDtypeStruct((28, ROWS, NZ), jnp.bfloat16)),
        in_specs=[smem] + [vmem] * 3,
        out_specs=[vmem] * 4,
        scratch_shapes=[
            pltpu.VMEM((ROWS * OWN, NZ), f32),
            pltpu.VMEM((SPAN * NY, NZ), f32),
            pltpu.VMEM((64, ROWS, NZ), f32),
            pltpu.VMEM((52, ROWS, NZ), f32),
            pltpu.VMEM((40, ROWS, NZ), f32),
            pltpu.VMEM((28, ROWS, NZ), f32),
        ],
        compiler_params=pltpu.CompilerParams(vmem_limit_bytes=VMEM_LIMIT),
        cost_estimate=pl.CostEstimate(
            flops=2_000_000_000, bytes_accessed=8_000_000, transcendentals=0
        ),
        name="filter_inner",
    )(scal, own, v_own, z_both())


def outer_planes(scal, base, left, right, v_own, inner):
    smem = pl.BlockSpec(memory_space=pltpu.SMEM)
    vmem = pl.BlockSpec(memory_space=pltpu.VMEM)
    f32 = jnp.float32
    return pl.pallas_call(
        outer_kernel,
        out_shape=jax.ShapeDtypeStruct((OWN // SLAB, SENT, ROWS, NZ), jnp.bfloat16),
        in_specs=[smem, smem] + [vmem] * 8,
        out_specs=vmem,
        scratch_shapes=[
            pltpu.VMEM(left.shape, f32),
            pltpu.VMEM((SPAN * NY, NZ), f32),
            pltpu.VMEM((36, ROWS, NZ), f32),
            pltpu.VMEM((36, ROWS, NZ), f32),
            pltpu.VMEM((36, ROWS, NZ), f32),
            pltpu.VMEM((70, ROWS, NZ), f32),
        ],
        compiler_params=pltpu.CompilerParams(vmem_limit_bytes=VMEM_LIMIT),
        name="filter_outer",
    )(scal, base, left, right, v_own, *inner, z_both())


def sums_kernel(planes, v, kz, out, fields_out, cells_f, total):
    def unpack(x, carry):
        for g in range(BANDS // GROUP):
            part = planes[g, x].astype(jnp.float32).reshape(NY, GROUP, NZ)
            cells_f[x, :, pl.ds(g * GROUP, GROUP), :] = part
        return carry

    lax.fori_loop(0, SENT, unpack, 0)
    total[...] = jnp.zeros_like(total)

    def step(t, carry):
        x0 = t * PLANES
        block = cells_f[pl.ds(x0, PLANES)].reshape(PLANES * NY * BANDS, NZ)
        block16 = block.astype(jnp.bfloat16)
        z = jnp.dot(block16, kz[...], preferred_element_type=jnp.float32)
        add = total[...]
        for p in range(PLANES):
            x = x0 + p
            at = [slice((p * NY + y) * BANDS, (p * NY + y + 1) * BANDS) for y in range(NY)]
            images = []
            for y in range(NY):
                image = None
                for k in range(1, 7):
                    pair = cells_f[x + k, y]
                    if y + k < NY:
                        pair = pair + block[at[y + k]]
                    pair = SIDE[k - 1] * pair
                    image = pair if image is None else image + pair
                local = jnp.broadcast_to(v[x, pl.ds(y, 1), :], (BANDS, NZ))
                image = image + (0.5 * (local + CENTRE)) * block[at[y]]
                images.append(split_bf16(image + (z[at[y], :NZ] + z[at[y], NZ:])))
            fields = jnp.concatenate([block16[a] for a in at], axis=1)
            fields_out[x] = fields
            highs = jnp.concatenate([i[0] for i in images], axis=1)
            lows = jnp.concatenate([i[1] for i in images], axis=1)
            add = add + lax.dot_general(
                jnp.concatenate([fields, highs, lows], axis=0), fields,
                (((1,), (1,)), ((), ())), preferred_element_type=jnp.float32,
            )
        total[...] = add
        return carry

    lax.fori_loop(0, SLAB // PLANES, step, 0)
    sums = total[...]
    gram = sums[:BANDS]
    half = sums[BANDS : 2 * BANDS] + sums[2 * BANDS :]
    both = jnp.concatenate([gram, half], axis=1)
    row = jnp.concatenate([both[:16], both[16:]], axis=1)
    for copy in range(out.shape[0]):
        out[copy] = row


def matrix_sums(planes, v, copies):
    kz = jnp.asarray(np.concatenate(z_matrix(1), axis=1))
    vmem = pl.BlockSpec(memory_space=pltpu.VMEM)
    f32 = jnp.float32
    return pl.pallas_call(
        sums_kernel,
        out_shape=(
            jax.ShapeDtypeStruct((copies, 16, NZ), f32),
            jax.ShapeDtypeStruct((SLAB, BANDS, NY * NZ), jnp.bfloat16),
        ),
        in_specs=[vmem] * 3,
        out_specs=(vmem, vmem),
        scratch_shapes=[
            pltpu.VMEM((SENT, NY, BANDS, NZ), f32),
            pltpu.VMEM((3 * BANDS, BANDS), f32),
        ],
        compiler_params=pltpu.CompilerParams(vmem_limit_bytes=VMEM_LIMIT),
        name="matrix_sums",
    )(planes, v, kz)


def rotate_kernel(count, parts, fields, out, projected, turned):
    sums = jnp.sum(parts[...], axis=0) * (1.0 / count)
    gram = jnp.concatenate([sums[:, :32], sums[:, 64:96]], axis=0)
    half = jnp.concatenate([sums[:, 32:64], sums[:, 96:]], axis=0)
    ham = half + half.T
    rows = lax.broadcasted_iota(jnp.int32, (BANDS, BANDS), 0)
    columns = lax.broadcasted_iota(jnp.int32, (BANDS, BANDS), 1)
    unit = jnp.where(rows == columns, 1.0, 0.0).astype(jnp.float32)
    work = jnp.concatenate([gram, unit], axis=1)
    index = lax.broadcasted_iota(jnp.int32, (BANDS, 1), 0)
    def column(k):
        return jnp.broadcast_to(work[:, k : k + 1], (BANDS, 2 * BANDS))

    now, after = column(0), column(1)
    for k in range(BANDS):
        inverse_pivot = 1.0 / now[k : k + 1]
        lower = jnp.where(index > k, now, 0.0)
        work = work - lower * (work[k : k + 1] * inverse_pivot)
        if k + 1 < BANDS:
            now = after - lower * (after[k : k + 1] * inverse_pivot)
        if k + 2 < BANDS:
            after = column(k + 2)
    pivots = jnp.sum(jnp.where(rows == columns, work[:, :BANDS], 0.0), axis=1, keepdims=True)
    inverse = work[:, BANDS:] / jnp.sqrt(pivots)
    high = lax.Precision.HIGHEST
    left = jnp.dot(inverse, ham, precision=high, preferred_element_type=jnp.float32)
    projected[...] = lax.dot_general(
        left, inverse, (((1,), (1,)), ((), ())), precision=high,
        preferred_element_type=jnp.float32,
    )
    both = jnp.concatenate(split_bf16(inverse), axis=1)

    def turn(x, carry):
        data = fields[x]
        data = jnp.concatenate([data, data], axis=0)
        result = jnp.dot(both, data, preferred_element_type=jnp.float32)
        for y in range(NY):
            start = pl.multiple_of((x * NY + y) * BANDS, BANDS)
            turned[pl.ds(start, BANDS), :] = result[:, y * NZ : (y + 1) * NZ]
        return carry

    lax.fori_loop(0, SLAB, turn, 0)

    def give(b, carry):
        for pair in range(NY // 2):
            for g in range(BANDS // GROUP):
                for odd in range(2):
                    start = (2 * pair + odd) * BANDS + g * GROUP + b
                    value = turned[pl.ds(start, SLAB, stride=NY * BANDS), :]
                    out[(pair * GROUP + b) * (BANDS // GROUP) + g, odd] = value.astype(jnp.bfloat16)
        return carry

    lax.fori_loop(0, GROUP, give, 0)


def rotated_planes(parts, fields, count):
    vmem = pl.BlockSpec(memory_space=pltpu.VMEM)

    def kernel(*refs):
        rotate_kernel(count, *refs)

    return pl.pallas_call(
        kernel,
        out_shape=(
            jax.ShapeDtypeStruct((128, 2, SLAB, NZ), jnp.bfloat16),
            jax.ShapeDtypeStruct((BANDS, BANDS), jnp.float32),
        ),
        in_specs=[vmem] * 2,
        out_specs=(vmem, vmem),
        scratch_shapes=[pltpu.VMEM((SLAB * NY * BANDS, NZ), jnp.float32)],
        compiler_params=pltpu.CompilerParams(vmem_limit_bytes=VMEM_LIMIT),
        name="rotate_planes",
    )(parts, fields)


def local(orbitals, potential, cutoff, ceiling):
    x_cells = orbitals.shape[1]
    block_count = x_cells // OWN
    center = 0.5 * (ceiling[0] + cutoff[0])
    half_width = 0.5 * (ceiling[0] - cutoff[0])
    scal = jnp.stack([2.0 / half_width, CENTRE - center])
    block_index = lax.axis_index(BLOCKS)
    base = jnp.stack([block_index * OWN - HALO, jnp.int32(x_cells)])
    place = [z * 4 + y for y in range(4) for z in range(8)]
    up = [(place[i], place[i + 1]) for i in range(block_count - 1)]
    down = [(b, a) for a, b in up]

    x_index = lax.axis_index("x")
    slabs = [
        lax.ppermute(
            potential,
            ("x", "y"),
            [(y * 4 + (x + j) % 4, x * 4 + y) for x in range(4) for y in range(4)],
        )
        for j in range(4)
    ]
    v_slab = slabs[0]
    v_own = lax.dynamic_slice_in_dim(
        jnp.concatenate(slabs[1:] + slabs), (3 - x_index) * SLAB, OWN, axis=0
    )

    chunks = orbitals.reshape(2, block_count, OWN, NZ).swapaxes(0, 1)
    own = lax.all_to_all(chunks, BLOCKS, split_axis=0, concat_axis=0, tiled=True)
    def with_potential(field, v):
        parts = [p.reshape(HALO * NY, NZ) for p in split_bf16(v)]
        return jnp.concatenate([field.reshape(ROWS * HALO, NZ)] + parts, axis=0)

    tail = with_potential(own[:, :, OWN - HALO :], v_own[OWN - HALO :])
    head = with_potential(own[:, :, :HALO], v_own[:HALO])
    left = lax.ppermute(tail, ("z", "y"), up)
    right = lax.ppermute(head, ("z", "y"), down)
    v_rows = v_own.reshape(OWN * NY, NZ)
    inner = inner_planes(scal, own.reshape(ROWS * OWN, NZ), v_rows)
    filtered = outer_planes(scal, base, left, right, v_rows, inner)
    planes = lax.all_to_all(filtered, "x", split_axis=0, concat_axis=0, tiled=True)
    sums, fields = matrix_sums(planes, v_slab, 16)
    sums = lax.all_to_all(sums, ("x", "y"), split_axis=0, concat_axis=0, tiled=True)
    sums = jnp.broadcast_to(jnp.sum(sums, axis=0)[None], (8, 16, NZ))
    sums = lax.all_to_all(sums, "z", split_axis=0, concat_axis=0, tiled=True)
    rotated, projected = rotated_planes(sums, fields, x_cells * NY * NZ)
    returned = lax.all_to_all(rotated, ("y", "z", "x"), split_axis=0, concat_axis=0, tiled=True)
    returned = returned.swapaxes(0, 1).reshape(2, x_cells, NZ)
    return (returned, projected)


def solution(mesh):
    mesh = Mesh(mesh.devices.reshape(2, 4, 8, 4), ("spin",) + DOM)
    return jax.shard_map(
        local,
        mesh=mesh,
        in_specs=(
            P(("spin",) + DOM, None, None),
            P(("spin",) + DOM, None, None),
            P("spin"),
            P("spin"),
        ),
        out_specs=(P(("spin",) + DOM, None, None), P("spin", None)),
        check_vma=False,
    )
```

time: 182 us -> 154 us (0.85)
  Pallas kernels: 39.8 us -> 23.7 us
  blocking collectives: 83.1 us -> 76.4 us
  waiting for transfers between devices: 25.5 us -> 20.9 us
    pallas_call x2 -> x3, Pallas kernels: 32.2 us -> 17.7 us  [the longest x1 7.69 us: inner_planes(): pl.pallas_call(inner_kernel, out_shape=(edge, edge, edge, jax.ShapeDtypeS...]
    all_gather x1 -> x0, blocking collectives: 12.3 us -> none  [local(): v_own = lax.all_gather(v_slab, 'x', tiled=True)]
    all_to_all x1, waiting for transfers between devices: 23.4 us -> 14.9 us  [local(): lax.all_to_all(chunks, BLOCKS, split_axis=0, concat_axis=0, tiled=True)]
    ppermute x5 -> x6, waiting for transfers between devices: 2.12 us -> 5.97 us  [the longest x1 3.1 us: local(): right = lax.ppermute(head, ('z', 'y'), down)]
    all_to_all x1, blocking collectives: 26.9 us -> 30.4 us  [local(): lax.all_to_all(rotated, ('y', 'z', 'x'), split_axis=0, concat_axis=0, til...]
    all_to_all x1, blocking collectives: 16 us -> 19.2 us  [local(): lax.all_to_all(filtered, 'x', split_axis=0, concat_axis=0, tiled=True)]
    all_to_all x1, blocking collectives: 16.4 us -> 13.6 us  [local(): lax.all_to_all(sums, ('x', 'y'), split_axis=0, concat_axis=0, tiled=True)]
    ppermute x5 -> x6, starting transfers between devices: 15.2 us -> 14.3 us  [the longest x4 9.29 us: local(): lax.ppermute(potential, ('x', 'y'), [(y * 4 + (x + j) % 4, x * 4 + y) for...]
  transfers between devices with their start and end apart: 6 -> 7, of which waited for: 3 -> 3; matrix products, arithmetic and copies ran while one was open for 0% -> 0% of each run, Pallas kernels for 0% -> 5%
where the time goes in v3:
time: 154 us; the launch traced here: 153 us
  blocking collectives  76.4 us (50%)
  starting transfers between devices  25.9 us (17%)
  Pallas kernels  23.7 us (15%)
  waiting for transfers between devices  20.9 us (14%)
  local copies, waits for them, and re-layouts  3.64 us (2%)
  between operations  2.21 us (1%)
    all_to_all x1, blocking collectives, local(): lax.all_to_all(rotated, ('y', 'z', 'x'), split_axis=0, concat_axis=0, til...  30.4 us
    all_to_all x1, blocking collectives, local(): lax.all_to_all(filtered, 'x', split_axis=0, concat_axis=0, tiled=True)  19.2 us
    all_to_all x1, waiting for transfers between devices, local(): lax.all_to_all(chunks, BLOCKS, split_axis=0, concat_axis=0, tiled=True)  14.9 us
    all_to_all x1, blocking collectives, local(): lax.all_to_all(sums, ('x', 'y'), split_axis=0, concat_axis=0, tiled=True)  13.6 us
    all_to_all x1, blocking collectives, local(): sums = lax.all_to_all(sums, 'z', split_axis=0, concat_axis=0, tiled=True)  13.2 us
    all_to_all x1, starting transfers between devices, local(): lax.all_to_all(chunks, BLOCKS, split_axis=0, concat_axis=0, tiled=True)  11.6 us
    ppermute x4, starting transfers between devices, local(): lax.ppermute(potential, ('x', 'y'), [(y * 4 + (x + j) % 4, x * 4 + y) for...  9.29 us
    pallas_call x1, Pallas kernels, inner_planes(): pl.pallas_call(inner_kernel, out_shape=(edge, edge, edge, jax.ShapeDtypeS...  7.69 us
  transfers between devices with their start and end apart: 7, of which 3 were waited for; matrix products, arithmetic and copies ran while one was open for 0% of the time, Pallas kernels for 5%

profile of v3, /device:TPU:2, one launch (start us, length us, event | category | flops | bytes accessed | tf_op | source)
XLA Modules:
  0.0 153.0 jit_solution(15537245305796858096)
XLA Ops:
  0.6 2.3 %copy.13 = bf16[2,32,64,128]{3,2,0,1:T(8,128)(2,1)} copy(bf16[2,32,64,128]{3,2,1,0:T(8,128)(2,1)} %bitcast.24) | data formatting | bytes 2097152 | tf_op jit(solution)/shard_map/reshape | solution.py:389
  2.9 0.0 copy-start.2
  2.9 11.6 %all-to-all-start = ((bf16[32,2,64,128]{3,2,1,0:T(8,128)(2,1)}), bf16[32,2,64,128]{3,2,1,0:T(8,128)(2,1)S(1)}, u32[]{:S(2)}, u32[]{:S(2)}) async-start(bf16[32,2,64,128]{3,2,1,0:T(8,128)(2,1)} %bitcast.19), calls=%async_computation | async-start | bytes 2097152 | tf_op jit(solution)/shard_map/all_to_all | solution.py:390
  14.5 0.0 copy-done.2
  14.6 3.4 %collective-permute-start = (f32[16,8,128]{2,1,0:T(8,128)S(1)}, f32[16,8,128]{2,1,0:T(8,128)S(1)}, u32[]{:S(2)}, u32[]{:S(2)}) collective-permute-start(f32[16,8,128]{2,1,0:T(8,128)S(1)} %copy-done.2), channel_id=1, source_target_pairs={{1,0},{33,1},{65,2},{97,3},{2,32},{34,33},{66,34},{98,35},{3,64},{... | collective-permute-start | bytes 196616 | tf_op jit(solution)/shard_map/ppermute | solution.py:377
  18.0 0.8 collective-permute-start.1
  18.8 5.0 %collective-permute-start.3 = (f32[16,8,128]{2,1,0:T(8,128)S(1)}, f32[16,8,128]{2,1,0:T(8,128)S(1)}, u32[]{:S(2)}, u32[]{:S(2)}) collective-permute-start(f32[16,8,128]{2,1,0:T(8,128)S(1)} %copy-done.2), channel_id=1, source_target_pairs={{0,0},{32,1},{64,2},{96,3},{1,32},{33,33},{65,34},{97,35},{2,64},{... | collective-permute-start | bytes 196616 | tf_op jit(solution)/shard_map/ppermute | solution.py:377
  23.8 0.1 collective-permute-start.2
  25.2 0.0 collective-permute-done
  25.2 0.0 collective-permute-done.1
  25.3 2.9 %collective-permute-done.2 = f32[16,8,128]{2,1,0:T(8,128)S(1)} collective-permute-done((f32[16,8,128]{2,1,0:T(8,128)S(1)}, f32[16,8,128]{2,1,0:T(8,128)S(1)}, u32[]{:S(2)}, u32[]{:S(2)}) %collective-permute-start.2) | collective-permute-done | bytes 65568 | tf_op jit(solution)/shard_map/ppermute | solution.py:377
  28.1 0.0 collective-permute-done.3.v
  28.3 14.9 %all-to-all-done = bf16[32,2,64,128]{3,2,1,0:T(8,128)(2,1)S(1)} async-done(((bf16[32,2,64,128]{3,2,1,0:T(8,128)(2,1)}), bf16[32,2,64,128]{3,2,1,0:T(8,128)(2,1)S(1)}, u32[]{:S(2)}, u32[]{:S(2)}) %all-to-all-start) | async-done | bytes 1048608 | tf_op jit(solution)/shard_map/all_to_all | solution.py:390
  43.2 0.1 fusion.4
  43.3 0.0 copy-start
  43.3 3.7 %collective-permute-start.4 = (bf16[1920,128]{1,0:T(8,128)(2,1)S(1)}, bf16[1920,128]{1,0:T(8,128)(2,1)S(1)}, u32[]{:S(2)}, u32[]{:S(2)}) collective-permute-start(bf16[1920,128]{1,0:T(8,128)(2,1)S(1)} %pad_maximum_fusion), channel_id=1, source_target_pairs={{0,4},{4,8},{8,12},{12,16},{16,20},{20,24},{24,28},{28,1},{1,5},{5... | collective-permute-start | bytes 1474568 | tf_op jit(solution)/shard_map/ppermute | solution.py:397
  47.1 1.3 collective-permute-start.5
  48.4 0.1 pad_maximum_fusion.2.scal
  48.5 0.1 pad_add_fusion.base
  48.6 0.0 copy-done
  48.6 7.7 %filter_inner.1 = (f32[2,12,64,128]{3,2,1,0:T(8,128)S(1)}, f32[2,12,64,128]{3,2,1,0:T(8,128)S(1)}, f32[2,12,64,128]{3,2,1,0:T(8,128)S(1)}, bf16[28,64,128]{2,1,0:T(8,128)(2,1)S(1)}) custom-call(f32[2]{0:T(128)S(1)} %pad_maximum_fusion.2.scal, bf16[4096,128]{1,0:T(8,128)(2,1)S(1)} %bitcast.20, f32[512,128]{1,0:T(8,128)S(1)} %dynamic-slice_bitcast_fusion.v_own, ...), custom_call_target="tpu_custom_call" | custom-call | flops 2000000000 | bytes 8000000 | tf_op jit(solution)/shard_map/filter_inner/pallas_call | solution.py:172
  56.3 0.0 collective-permute-done.4.left
  56.3 3.1 %collective-permute-done.5.right = bf16[1920,128]{1,0:T(8,128)(2,1)S(1)} collective-permute-done((bf16[1920,128]{1,0:T(8,128)(2,1)S(1)}, bf16[1920,128]{1,0:T(8,128)(2,1)S(1)}, u32[]{:S(2)}, u32[]{:S(2)}) %collective-permute-start.5) | collective-permute-done | bytes 491552 | tf_op jit(solution)/shard_map/ppermute | solution.py:398
  59.4 7.4 %filter_outer.1 = bf16[4,22,64,128]{3,2,1,0:T(8,128)(2,1)S(1)} custom-call(f32[2]{0:T(128)S(1)} %pad_maximum_fusion.2.scal, s32[2]{0:T(128)S(1)} %pad_add_fusion.base, bf16[1920,128]{1,0:T(8,128)(2,1)S(1)} %collective-permute-done.4.left, bf16[1920,128]{1,0:T(8,128)(2,1)S(1)} %collective-permute-done.5.right, ...), custom_call_target="tpu_custom_call" | custom-call | tf_op jit(solution)/shard_map/filter_outer/pallas_call | solution.py:197
  66.9 0.0 copy-start.1
  66.9 19.2 %all_to_all.25.planes = bf16[4,22,64,128]{3,2,1,0:T(8,128)(2,1)S(1)} all-to-all(bf16[4,22,64,128]{3,2,1,0:T(8,128)(2,1)S(1)} %filter_outer.1), channel_id=1, replica_groups=mesh['spin'=2,'x'=4,'z'=8,'y'=4] {'x'}, dimensions={0} | all-to-all | bytes 2883584 | tf_op jit(solution)/shard_map/all_to_all | solution.py:402
  86.1 0.0 copy-done.1
  86.1 2.6 %matrix_sums.1 = (f32[16,16,128]{2,1,0:T(8,128)S(1)}, bf16[16,32,1024]{2,1,0:T(8,128)(2,1)S(1)}) custom-call(bf16[4,22,64,128]{3,2,1,0:T(8,128)(2,1)S(1)} %all_to_all.25.planes, f32[16,8,128]{2,1,0:T(8,128)S(1)} %collective-permute-done.3.v, bf16[128,256]{1,0:T(8,128)(2,1)S(1)} %copy-done.1), custom_call_target="tpu_custom_call" | custom-call | tf_op jit(solution)/shard_map/matrix_sums/pallas_call | solution.py:271
  88.7 13.6 %all_to_all.26 = f32[16,16,128]{2,1,0:T(8,128)S(1)} all-to-all(f32[16,16,128]{2,1,0:T(8,128)S(1)} %get-tuple-element.14), channel_id=1, replica_groups=mesh['spin'=2,'x'=4,'z'=8,'y'=4] {'x','y'}, dimensions={0} | all-to-all | bytes 262144 | tf_op jit(solution)/shard_map/all_to_all | solution.py:404
  102.3 13.2 %all_to_all.27.refs_0_ = f32[8,16,128]{2,1,0:T(8,128)S(1)} all-to-all(f32[8,16,128]{2,1,0:T(8,128)S(1)} %broadcast_in_dim.2), channel_id=1, replica_groups=mesh['spin'=2,'x'=4,'z'=8,'y'=4] {'z'}, dimensions={0} | all-to-all | bytes 131072 | tf_op jit(solution)/shard_map/all_to_all | solution.py:406
  115.5 6.0 %rotate_planes.1 = (bf16[128,2,16,128]{3,2,1,0:T(8,128)(2,1)S(1)}, f32[32,32]{1,0:T(8,128)}) custom-call(f32[8,16,128]{2,1,0:T(8,128)S(1)} %all_to_all.27.refs_0_, bf16[16,32,1024]{2,1,0:T(8,128)(2,1)S(1)} %get-tuple-element.15.refs_1_), custom_call_target="tpu_custom_call" | custom-call | tf_op jit(solution)/shard_map/rotate_planes/pallas_call | solution.py:349
  121.5 30.4 %all_to_all.28 = bf16[128,2,16,128]{3,2,1,0:T(8,128)(2,1)S(1)} all-to-all(bf16[128,2,16,128]{3,2,1,0:T(8,128)(2,1)S(1)} %get-tuple-element.16), channel_id=1, replica_groups=mesh['spin'=2,'x'=4,'z'=8,'y'=4] {'y','z','x'}, dimensions={0} | all-to-all | bytes 2097152 | tf_op jit(solution)/shard_map/all_to_all | solution.py:408
  151.8 1.1 copy.11
  (14 shorter events, 0.2 us)
Async XLA Ops:
  2.9 11.6 %copy-start.2 = (f32[16,8,128]{2,1,0:T(8,128)S(1)}, f32[16,8,128]{2,1,0:T(8,128)}, u32[]{:S(2)}) copy-start(f32[16,8,128]{2,1,0:T(8,128)} %param.8) | copy-start | bytes 196612
  2.9 40.3 %all-to-all-start = ((bf16[32,2,64,128]{3,2,1,0:T(8,128)(2,1)}), bf16[32,2,64,128]{3,2,1,0:T(8,128)(2,1)S(1)}, u32[]{:S(2)}, u32[]{:S(2)}) async-start(bf16[32,2,64,128]{3,2,1,0:T(8,128)(2,1)} %bitcast.19), calls=%async_computation | async-start | bytes 2097152 | tf_op jit(solution)/shard_map/all_to_all | solution.py:390
  14.6 10.7 %collective-permute-start = (f32[16,8,128]{2,1,0:T(8,128)S(1)}, f32[16,8,128]{2,1,0:T(8,128)S(1)}, u32[]{:S(2)}, u32[]{:S(2)}) collective-permute-start(f32[16,8,128]{2,1,0:T(8,128)S(1)} %copy-done.2), channel_id=1, source_target_pairs={{1,0},{33,1},{65,2},{97,3},{2,32},{34,33},{66,34},{98,35},{3,64},{... | collective-permute-start | bytes 196616 | tf_op jit(solution)/shard_map/ppermute | solution.py:377
  18.0 7.2 %collective-permute-start.1 = (f32[16,8,128]{2,1,0:T(8,128)S(1)}, f32[16,8,128]{2,1,0:T(8,128)S(1)}, u32[]{:S(2)}, u32[]{:S(2)}) collective-permute-start(f32[16,8,128]{2,1,0:T(8,128)S(1)} %copy-done.2), channel_id=1, source_target_pairs={{2,0},{34,1},{66,2},{98,3},{3,32},{35,33},{67,34},{99,35},{0,64},{... | collective-permute-start | bytes 196616 | tf_op jit(solution)/shard_map/ppermute | solution.py:377
  18.8 9.4 %collective-permute-start.3 = (f32[16,8,128]{2,1,0:T(8,128)S(1)}, f32[16,8,128]{2,1,0:T(8,128)S(1)}, u32[]{:S(2)}, u32[]{:S(2)}) collective-permute-start(f32[16,8,128]{2,1,0:T(8,128)S(1)} %copy-done.2), channel_id=1, source_target_pairs={{0,0},{32,1},{64,2},{96,3},{1,32},{33,33},{65,34},{97,35},{2,64},{... | collective-permute-start | bytes 196616 | tf_op jit(solution)/shard_map/ppermute | solution.py:377
  23.8 4.3 %collective-permute-start.2 = (f32[16,8,128]{2,1,0:T(8,128)S(1)}, f32[16,8,128]{2,1,0:T(8,128)S(1)}, u32[]{:S(2)}, u32[]{:S(2)}) collective-permute-start(f32[16,8,128]{2,1,0:T(8,128)S(1)} %copy-done.2), channel_id=1, source_target_pairs={{3,0},{35,1},{67,2},{99,3},{0,32},{32,33},{64,34},{96,35},{1,64},{... | collective-permute-start | bytes 196616 | tf_op jit(solution)/shard_map/ppermute | solution.py:377
  43.3 5.3 %copy-start = (bf16[256,256]{1,0:T(8,128)(2,1)S(1)}, bf16[256,256]{1,0:T(8,128)(2,1)}, u32[]{:S(2)}) copy-start(bf16[256,256]{1,0:T(8,128)(2,1)} %constant.46.clone.kz) | copy-start | bytes 393220
  43.3 13.0 %collective-permute-start.4 = (bf16[1920,128]{1,0:T(8,128)(2,1)S(1)}, bf16[1920,128]{1,0:T(8,128)(2,1)S(1)}, u32[]{:S(2)}, u32[]{:S(2)}) collective-permute-start(bf16[1920,128]{1,0:T(8,128)(2,1)S(1)} %pad_maximum_fusion), channel_id=1, source_target_pairs={{0,4},{4,8},{8,12},{12,16},{16,20},{20,24},{24,28},{28,1},{1,5},{5... | collective-permute-start | bytes 1474568 | tf_op jit(solution)/shard_map/ppermute | solution.py:397
  47.1 12.3 %collective-permute-start.5 = (bf16[1920,128]{1,0:T(8,128)(2,1)S(1)}, bf16[1920,128]{1,0:T(8,128)(2,1)S(1)}, u32[]{:S(2)}, u32[]{:S(2)}) collective-permute-start(bf16[1920,128]{1,0:T(8,128)(2,1)S(1)} %pad_maximum_fusion.1), channel_id=1, source_target_pairs={{4,0},{8,4},{12,8},{16,12},{20,16},{24,20},{28,24},{1,28},{5,1},{9... | collective-permute-start | bytes 1474568 | tf_op jit(solution)/shard_map/ppermute | solution.py:398
  66.9 19.2 %copy-start.1 = (bf16[128,256]{1,0:T(8,128)(2,1)S(1)}, bf16[128,256]{1,0:T(8,128)(2,1)}, u32[]{:S(2)}) copy-start(bf16[128,256]{1,0:T(8,128)(2,1)} %constant.47.clone.kz) | copy-start | bytes 196612

commit v4 on v3

--- a/solution.py
+++ b/solution.py
@@ -6,8 +6,8 @@
 from jax.experimental.pallas import tpu as pltpu
 from jax.sharding import Mesh, PartitionSpec as P
 
-DOM = ("x", "z", "y")
-BLOCKS = ("y", "z")
+DOM = ("x", "h", "l", "y")
+BLOCKS = ("y", "h", "l")
 
 STENCIL = (
     -5369.0 / 1800.0,
@@ -119,9 +119,9 @@
     u[pl.ds(HALO * NY, OWN * NY)] = (v_own[...] + scal[1]) * scale
     own_f[...] = own[...].astype(jnp.float32)
     bring(own_f, OWN, s, 0)
-    level(kz, u, scale, None, s, 24, None, 0, y1, 30, 30, 82, 13, start=True)
-    level(kz, u, scale, None, y1, 30, s, 24, y2, 36, 36, 76, 10)
-    level(kz, u, scale, None, y2, 36, y1, 30, y3, 42, 42, 70, 14)
+    level(kz, u, scale, None, s, 24, None, 0, y1, 30, 30, 82, 26, start=True)
+    level(kz, u, scale, None, y1, 30, s, 24, y2, 36, 36, 76, 20)
+    level(kz, u, scale, None, y2, 36, y1, 30, y3, 42, 42, 70, 28)
     for ref, edge in ((s, s_edge), (y1, y1_edge), (y2, y2_edge)):
         edge[0] = ref[pl.ds(0, EDGE)]
         edge[1] = ref[pl.ds(ref.shape[0] - EDGE, EDGE)]
@@ -148,13 +148,13 @@
         y1[pl.ds(y1_at, EDGE)] = y1_edge[side]
         y2[pl.ds(y2_at, EDGE)] = y2_edge[side]
         if side == 0:
-            level(kz, u, scale, base, s, 0, None, 0, y1, 12, 12, 30, 9, start=True)
-            level(kz, u, scale, base, y1, 12, s, 0, y2, 18, 18, 36, 9)
-            level(kz, u, scale, base, y2, 18, y1, 12, y3, 24, 24, 42, 9)
+            level(kz, u, scale, base, s, 0, None, 0, y1, 12, 12, 30, 18, start=True)
+            level(kz, u, scale, base, y1, 12, s, 0, y2, 18, 18, 36, 18)
+            level(kz, u, scale, base, y2, 18, y1, 12, y3, 24, 24, 42, 18)
         else:
-            level(kz, u, scale, base, s, 76, None, 0, y1, 70, 82, 106, 12, start=True)
-            level(kz, u, scale, base, y1, 70, s, 76, y2, 64, 76, 100, 12)
-            level(kz, u, scale, base, y2, 64, y1, 70, y3, 24, 70, 94, 12)
+            level(kz, u, scale, base, s, 76, None, 0, y1, 70, 82, 106, 24, start=True)
+            level(kz, u, scale, base, y1, 70, s, 76, y2, 64, 76, 100, 24)
+            level(kz, u, scale, base, y2, 64, y1, 70, y3, 24, 70, 94, 24)
     for dest in range(OWN // SLAB):
         out[dest] = y3[pl.ds(dest * SLAB, SENT)].astype(jnp.bfloat16)
 
@@ -329,12 +329,13 @@
     lax.fori_loop(0, SLAB, turn, 0)
 
     def give(b, carry):
+        owner = (lax.rem(b, 4) * 2 + lax.div(b, 4)) * 16
         for pair in range(NY // 2):
             for g in range(BANDS // GROUP):
                 for odd in range(2):
                     start = (2 * pair + odd) * BANDS + g * GROUP + b
                     value = turned[pl.ds(start, SLAB, stride=NY * BANDS), :]
-                    out[(pair * GROUP + b) * (BANDS // GROUP) + g, odd] = value.astype(jnp.bfloat16)
+                    out[owner + pair * 4 + g, odd] = value.astype(jnp.bfloat16)
         return carry
 
     lax.fori_loop(0, GROUP, give, 0)
@@ -394,8 +395,8 @@
 
     tail = with_potential(own[:, :, OWN - HALO :], v_own[OWN - HALO :])
     head = with_potential(own[:, :, :HALO], v_own[:HALO])
-    left = lax.ppermute(tail, ("z", "y"), up)
-    right = lax.ppermute(head, ("z", "y"), down)
+    left = lax.ppermute(tail, ("h", "l", "y"), up)
+    right = lax.ppermute(head, ("h", "l", "y"), down)
     v_rows = v_own.reshape(OWN * NY, NZ)
     inner = inner_planes(scal, own.reshape(ROWS * OWN, NZ), v_rows)
     filtered = outer_planes(scal, base, left, right, v_rows, inner)
@@ -403,15 +404,18 @@
     sums, fields = matrix_sums(planes, v_slab, 16)
     sums = lax.all_to_all(sums, ("x", "y"), split_axis=0, concat_axis=0, tiled=True)
     sums = jnp.broadcast_to(jnp.sum(sums, axis=0)[None], (8, 16, NZ))
-    sums = lax.all_to_all(sums, "z", split_axis=0, concat_axis=0, tiled=True)
+    sums = lax.all_to_all(sums, ("l", "h"), split_axis=0, concat_axis=0, tiled=True)
     rotated, projected = rotated_planes(sums, fields, x_cells * NY * NZ)
-    returned = lax.all_to_all(rotated, ("y", "z", "x"), split_axis=0, concat_axis=0, tiled=True)
-    returned = returned.swapaxes(0, 1).reshape(2, x_cells, NZ)
+    returned = lax.all_to_all(
+        rotated, ("l", "h", "y", "x"), split_axis=0, concat_axis=0, tiled=True
+    )
+    returned = returned.reshape(4, 2, 4, 4, 2, SLAB, NZ).transpose(4, 2, 1, 0, 3, 5, 6)
+    returned = returned.reshape(2, x_cells, NZ)
     return (returned, projected)
 
 
 def solution(mesh):
-    mesh = Mesh(mesh.devices.reshape(2, 4, 8, 4), ("spin",) + DOM)
+    mesh = Mesh(mesh.devices.reshape(2, 4, 2, 4, 4), ("spin",) + DOM)
     return jax.shard_map(
         local,
         mesh=mesh,

time: 154 us -> 153 us (level)
  no operation moved by 1% of the time
where the time goes in v4:
time: 153 us; the launch traced here: 151 us
  blocking collectives  75.5 us (49%)
  starting transfers between devices  26.1 us (17%)
  Pallas kernels  22.2 us (15%)
  waiting for transfers between devices  21.2 us (14%)
  local copies, waits for them, and re-layouts  3.77 us (2%)
  between operations  2.21 us (1%)
    all_to_all x1, blocking collectives, local(): lax.all_to_all(rotated, ('l', 'h', 'y', 'x'), split_axis=0, concat_axis=0...  30.1 us
    all_to_all x1, blocking collectives, local(): lax.all_to_all(filtered, 'x', split_axis=0, concat_axis=0, tiled=True)  19.2 us
    all_to_all x1, waiting for transfers between devices, local(): lax.all_to_all(chunks, BLOCKS, split_axis=0, concat_axis=0, tiled=True)  14.9 us
    all_to_all x1, blocking collectives, local(): lax.all_to_all(sums, ('x', 'y'), split_axis=0, concat_axis=0, tiled=True)  13.5 us
    all_to_all x1, blocking collectives, local(): lax.all_to_all(sums, ('l', 'h'), split_axis=0, concat_axis=0, tiled=True)  12.7 us
    all_to_all x1, starting transfers between devices, local(): lax.all_to_all(chunks, BLOCKS, split_axis=0, concat_axis=0, tiled=True)  11.6 us
    ppermute x4, starting transfers between devices, local(): lax.ppermute(potential, ('x', 'y'), [(y * 4 + (x + j) % 4, x * 4 + y) for...  9.29 us
    pallas_call x1, Pallas kernels, inner_planes(): pl.pallas_call(inner_kernel, out_shape=(edge, edge, edge, jax.ShapeDtypeS...  7.22 us
  transfers between devices with their start and end apart: 7, of which 3 were waited for; matrix products, arithmetic and copies ran while one was open for 0% of the time, Pallas kernels for 5%

profile of v4, /device:TPU:2, one launch (start us, length us, event | category | flops | bytes accessed | tf_op | source)
XLA Modules:
  0.0 151.2 jit_solution(18203258292150798164)
XLA Ops:
  0.6 2.3 %copy.12 = bf16[2,32,64,128]{3,2,0,1:T(8,128)(2,1)} copy(bf16[2,32,64,128]{3,2,1,0:T(8,128)(2,1)} %bitcast.26) | data formatting | bytes 2097152 | tf_op jit(solution)/shard_map/reshape | solution.py:390
  2.9 0.0 copy-start.2
  2.9 11.6 %all-to-all-start = ((bf16[32,2,64,128]{3,2,1,0:T(8,128)(2,1)}), bf16[32,2,64,128]{3,2,1,0:T(8,128)(2,1)S(1)}, u32[]{:S(2)}, u32[]{:S(2)}) async-start(bf16[32,2,64,128]{3,2,1,0:T(8,128)(2,1)} %bitcast.21), calls=%async_computation | async-start | bytes 2097152 | tf_op jit(solution)/shard_map/all_to_all | solution.py:391
  14.5 0.0 copy-done.2
  14.6 3.4 %collective-permute-start = (f32[16,8,128]{2,1,0:T(8,128)S(1)}, f32[16,8,128]{2,1,0:T(8,128)S(1)}, u32[]{:S(2)}, u32[]{:S(2)}) collective-permute-start(f32[16,8,128]{2,1,0:T(8,128)S(1)} %copy-done.2), channel_id=1, source_target_pairs={{1,0},{33,1},{65,2},{97,3},{2,32},{34,33},{66,34},{98,35},{3,64},{... | collective-permute-start | bytes 196616 | tf_op jit(solution)/shard_map/ppermute | solution.py:378
  18.0 0.8 collective-permute-start.1
  18.8 5.0 %collective-permute-start.3 = (f32[16,8,128]{2,1,0:T(8,128)S(1)}, f32[16,8,128]{2,1,0:T(8,128)S(1)}, u32[]{:S(2)}, u32[]{:S(2)}) collective-permute-start(f32[16,8,128]{2,1,0:T(8,128)S(1)} %copy-done.2), channel_id=1, source_target_pairs={{0,0},{32,1},{64,2},{96,3},{1,32},{33,33},{65,34},{97,35},{2,64},{... | collective-permute-start | bytes 196616 | tf_op jit(solution)/shard_map/ppermute | solution.py:378
  23.8 0.1 collective-permute-start.2
  25.2 0.0 collective-permute-done
  25.2 0.0 collective-permute-done.1
  25.3 2.9 %collective-permute-done.2 = f32[16,8,128]{2,1,0:T(8,128)S(1)} collective-permute-done((f32[16,8,128]{2,1,0:T(8,128)S(1)}, f32[16,8,128]{2,1,0:T(8,128)S(1)}, u32[]{:S(2)}, u32[]{:S(2)}) %collective-permute-start.2) | collective-permute-done | bytes 65568 | tf_op jit(solution)/shard_map/ppermute | solution.py:378
  28.1 0.0 collective-permute-done.3.v
  28.3 14.9 %all-to-all-done = bf16[32,2,64,128]{3,2,1,0:T(8,128)(2,1)S(1)} async-done(((bf16[32,2,64,128]{3,2,1,0:T(8,128)(2,1)}), bf16[32,2,64,128]{3,2,1,0:T(8,128)(2,1)S(1)}, u32[]{:S(2)}, u32[]{:S(2)}) %all-to-all-start) | async-done | bytes 1048608 | tf_op jit(solution)/shard_map/all_to_all | solution.py:391
  43.2 0.1 fusion.4
  43.3 0.0 copy-start
  43.3 3.7 %collective-permute-start.4 = (bf16[1920,128]{1,0:T(8,128)(2,1)S(1)}, bf16[1920,128]{1,0:T(8,128)(2,1)S(1)}, u32[]{:S(2)}, u32[]{:S(2)}) collective-permute-start(bf16[1920,128]{1,0:T(8,128)(2,1)S(1)} %pad_maximum_fusion), channel_id=1, source_target_pairs={{0,4},{4,8},{8,12},{12,16},{16,20},{20,24},{24,28},{28,1},{1,5},{5... | collective-permute-start | bytes 1474568 | tf_op jit(solution)/shard_map/ppermute | solution.py:398
  47.1 1.5 collective-permute-start.5
  48.6 0.1 pad_maximum_fusion.2.scal
  48.7 0.1 pad_add_fusion.base
  48.8 0.0 copy-done
  48.8 7.2 %filter_inner.1 = (f32[2,12,64,128]{3,2,1,0:T(8,128)S(1)}, f32[2,12,64,128]{3,2,1,0:T(8,128)S(1)}, f32[2,12,64,128]{3,2,1,0:T(8,128)S(1)}, bf16[28,64,128]{2,1,0:T(8,128)(2,1)S(1)}) custom-call(f32[2]{0:T(128)S(1)} %pad_maximum_fusion.2.scal, bf16[4096,128]{1,0:T(8,128)(2,1)S(1)} %bitcast.22, f32[512,128]{1,0:T(8,128)S(1)} %dynamic-slice_bitcast_fusion.v_own, ...), custom_call_target="tpu_custom_call" | custom-call | flops 2000000000 | bytes 8000000 | tf_op jit(solution)/shard_map/filter_inner/pallas_call | solution.py:172
  56.0 0.0 collective-permute-done.4.left
  56.0 3.4 %collective-permute-done.5.right = bf16[1920,128]{1,0:T(8,128)(2,1)S(1)} collective-permute-done((bf16[1920,128]{1,0:T(8,128)(2,1)S(1)}, bf16[1920,128]{1,0:T(8,128)(2,1)S(1)}, u32[]{:S(2)}, u32[]{:S(2)}) %collective-permute-start.5) | collective-permute-done | bytes 491552 | tf_op jit(solution)/shard_map/ppermute | solution.py:399
  59.4 6.3 %filter_outer.1 = bf16[4,22,64,128]{3,2,1,0:T(8,128)(2,1)S(1)} custom-call(f32[2]{0:T(128)S(1)} %pad_maximum_fusion.2.scal, s32[2]{0:T(128)S(1)} %pad_add_fusion.base, bf16[1920,128]{1,0:T(8,128)(2,1)S(1)} %collective-permute-done.4.left, bf16[1920,128]{1,0:T(8,128)(2,1)S(1)} %collective-permute-done.5.right, ...), custom_call_target="tpu_custom_call" | custom-call | tf_op jit(solution)/shard_map/filter_outer/pallas_call | solution.py:197
  65.7 0.0 copy-start.1
  65.7 19.2 %all_to_all.25.planes = bf16[4,22,64,128]{3,2,1,0:T(8,128)(2,1)S(1)} all-to-all(bf16[4,22,64,128]{3,2,1,0:T(8,128)(2,1)S(1)} %filter_outer.1), channel_id=1, replica_groups=mesh['spin'=2,'x'=4,'h'=2,'l'=4,'y'=4] {'x'}, dimensions={0} | all-to-all | bytes 2883584 | tf_op jit(solution)/shard_map/all_to_all | solution.py:403
  84.9 0.0 copy-done.1
  84.9 2.6 %matrix_sums.1 = (f32[16,16,128]{2,1,0:T(8,128)S(1)}, bf16[16,32,1024]{2,1,0:T(8,128)(2,1)S(1)}) custom-call(bf16[4,22,64,128]{3,2,1,0:T(8,128)(2,1)S(1)} %all_to_all.25.planes, f32[16,8,128]{2,1,0:T(8,128)S(1)} %collective-permute-done.3.v, bf16[128,256]{1,0:T(8,128)(2,1)S(1)} %copy-done.1), custom_call_target="tpu_custom_call" | custom-call | tf_op jit(solution)/shard_map/matrix_sums/pallas_call | solution.py:271
  87.5 13.5 %all_to_all.26 = f32[16,16,128]{2,1,0:T(8,128)S(1)} all-to-all(f32[16,16,128]{2,1,0:T(8,128)S(1)} %get-tuple-element.14), channel_id=1, replica_groups=mesh['spin'=2,'x'=4,'h'=2,'l'=4,'y'=4] {'x','y'}, dimensions={0} | all-to-all | bytes 262144 | tf_op jit(solution)/shard_map/all_to_all | solution.py:405
  101.1 12.7 %all_to_all.27.refs_0_ = f32[8,16,128]{2,1,0:T(8,128)S(1)} all-to-all(f32[8,16,128]{2,1,0:T(8,128)S(1)} %broadcast_in_dim.2), channel_id=1, replica_groups=mesh['spin'=2,'x'=4,'h'=2,'l'=4,'y'=4] {'l','h'}, dimensions={0} | all-to-all | bytes 131072 | tf_op jit(solution)/shard_map/all_to_all | solution.py:407
  113.8 6.1 %rotate_planes.1 = (bf16[128,2,16,128]{3,2,1,0:T(8,128)(2,1)S(1)}, f32[32,32]{1,0:T(8,128)}) custom-call(f32[8,16,128]{2,1,0:T(8,128)S(1)} %all_to_all.27.refs_0_, bf16[16,32,1024]{2,1,0:T(8,128)(2,1)S(1)} %get-tuple-element.15.refs_1_), custom_call_target="tpu_custom_call" | custom-call | tf_op jit(solution)/shard_map/rotate_planes/pallas_call | solution.py:350
  119.9 30.1 %all_to_all.28 = bf16[128,2,16,128]{3,2,1,0:T(8,128)(2,1)S(1)} all-to-all(bf16[128,2,16,128]{3,2,1,0:T(8,128)(2,1)S(1)} %get-tuple-element.16), channel_id=1, replica_groups=mesh['spin'=2,'x'=4,'h'=2,'l'=4,'y'=4] {'l','h','y','x'}, dimensions={0} | all-to-all | bytes 2097152 | tf_op jit(solution)/shard_map/all_to_all | solution.py:409
  150.0 1.3 copy.10
  (14 shorter events, 0.2 us)
Async XLA Ops:
  2.9 11.6 %copy-start.2 = (f32[16,8,128]{2,1,0:T(8,128)S(1)}, f32[16,8,128]{2,1,0:T(8,128)}, u32[]{:S(2)}) copy-start(f32[16,8,128]{2,1,0:T(8,128)} %param.8) | copy-start | bytes 196612
  2.9 40.3 %all-to-all-start = ((bf16[32,2,64,128]{3,2,1,0:T(8,128)(2,1)}), bf16[32,2,64,128]{3,2,1,0:T(8,128)(2,1)S(1)}, u32[]{:S(2)}, u32[]{:S(2)}) async-start(bf16[32,2,64,128]{3,2,1,0:T(8,128)(2,1)} %bitcast.21), calls=%async_computation | async-start | bytes 2097152 | tf_op jit(solution)/shard_map/all_to_all | solution.py:391
  14.6 10.7 %collective-permute-start = (f32[16,8,128]{2,1,0:T(8,128)S(1)}, f32[16,8,128]{2,1,0:T(8,128)S(1)}, u32[]{:S(2)}, u32[]{:S(2)}) collective-permute-start(f32[16,8,128]{2,1,0:T(8,128)S(1)} %copy-done.2), channel_id=1, source_target_pairs={{1,0},{33,1},{65,2},{97,3},{2,32},{34,33},{66,34},{98,35},{3,64},{... | collective-permute-start | bytes 196616 | tf_op jit(solution)/shard_map/ppermute | solution.py:378
  18.0 7.3 %collective-permute-start.1 = (f32[16,8,128]{2,1,0:T(8,128)S(1)}, f32[16,8,128]{2,1,0:T(8,128)S(1)}, u32[]{:S(2)}, u32[]{:S(2)}) collective-permute-start(f32[16,8,128]{2,1,0:T(8,128)S(1)} %copy-done.2), channel_id=1, source_target_pairs={{2,0},{34,1},{66,2},{98,3},{3,32},{35,33},{67,34},{99,35},{0,64},{... | collective-permute-start | bytes 196616 | tf_op jit(solution)/shard_map/ppermute | solution.py:378
  18.8 9.4 %collective-permute-start.3 = (f32[16,8,128]{2,1,0:T(8,128)S(1)}, f32[16,8,128]{2,1,0:T(8,128)S(1)}, u32[]{:S(2)}, u32[]{:S(2)}) collective-permute-start(f32[16,8,128]{2,1,0:T(8,128)S(1)} %copy-done.2), channel_id=1, source_target_pairs={{0,0},{32,1},{64,2},{96,3},{1,32},{33,33},{65,34},{97,35},{2,64},{... | collective-permute-start | bytes 196616 | tf_op jit(solution)/shard_map/ppermute | solution.py:378
  23.8 4.3 %collective-permute-start.2 = (f32[16,8,128]{2,1,0:T(8,128)S(1)}, f32[16,8,128]{2,1,0:T(8,128)S(1)}, u32[]{:S(2)}, u32[]{:S(2)}) collective-permute-start(f32[16,8,128]{2,1,0:T(8,128)S(1)} %copy-done.2), channel_id=1, source_target_pairs={{3,0},{35,1},{67,2},{99,3},{0,32},{32,33},{64,34},{96,35},{1,64},{... | collective-permute-start | bytes 196616 | tf_op jit(solution)/shard_map/ppermute | solution.py:378
  43.3 5.5 %copy-start = (bf16[256,256]{1,0:T(8,128)(2,1)S(1)}, bf16[256,256]{1,0:T(8,128)(2,1)}, u32[]{:S(2)}) copy-start(bf16[256,256]{1,0:T(8,128)(2,1)} %constant.52.clone.kz) | copy-start | bytes 393220
  43.3 12.7 %collective-permute-start.4 = (bf16[1920,128]{1,0:T(8,128)(2,1)S(1)}, bf16[1920,128]{1,0:T(8,128)(2,1)S(1)}, u32[]{:S(2)}, u32[]{:S(2)}) collective-permute-start(bf16[1920,128]{1,0:T(8,128)(2,1)S(1)} %pad_maximum_fusion), channel_id=1, source_target_pairs={{0,4},{4,8},{8,12},{12,16},{16,20},{20,24},{24,28},{28,1},{1,5},{5... | collective-permute-start | bytes 1474568 | tf_op jit(solution)/shard_map/ppermute | solution.py:398
  47.1 12.3 %collective-permute-start.5 = (bf16[1920,128]{1,0:T(8,128)(2,1)S(1)}, bf16[1920,128]{1,0:T(8,128)(2,1)S(1)}, u32[]{:S(2)}, u32[]{:S(2)}) collective-permute-start(bf16[1920,128]{1,0:T(8,128)(2,1)S(1)} %pad_maximum_fusion.1), channel_id=1, source_target_pairs={{4,0},{8,4},{12,8},{16,12},{20,16},{24,20},{28,24},{1,28},{5,1},{9... | collective-permute-start | bytes 1474568 | tf_op jit(solution)/shard_map/ppermute | solution.py:399
  65.7 19.2 %copy-start.1 = (bf16[128,256]{1,0:T(8,128)(2,1)S(1)}, bf16[128,256]{1,0:T(8,128)(2,1)}, u32[]{:S(2)}) copy-start(bf16[128,256]{1,0:T(8,128)(2,1)} %constant.53.clone.kz) | copy-start | bytes 196612

commit v5 on v4

--- a/solution.py
+++ b/solution.py
@@ -35,7 +35,7 @@
 ROWS = NY * GROUP
 EDGE = 12
 PLANES = 8
-VMEM_LIMIT = 48 * 1024 * 1024
+VMEM_LIMIT = 18 * 1024 * 1024
 
 
 def split_bf16(value):
@@ -139,7 +139,7 @@
     for side, halo in ((0, left), (1, right)):
         field_rows = ROWS * HALO
         side_f[...] = halo[...].astype(jnp.float32)
-        v = side_f[pl.ds(field_rows, v_rows)] + side_f[pl.ds(field_rows + v_rows, v_rows)]
+        v = side_f[pl.ds(field_rows, v_rows)]
         u[pl.ds(side * (HALO + OWN) * NY, v_rows)] = (v + scal[1]) * scale
         halo_at, edge_at = ((0, HALO), (EDGE, 0))[side]
         bring(side_f, HALO, s, halo_at)
@@ -326,7 +326,7 @@
             turned[pl.ds(start, BANDS), :] = result[:, y * NZ : (y + 1) * NZ]
         return carry
 
-    lax.fori_loop(0, SLAB, turn, 0)
+    lax.fori_loop(0, SLAB, turn, 0, unroll=4)
 
     def give(b, carry):
         owner = (lax.rem(b, 4) * 2 + lax.div(b, 4)) * 16
@@ -338,7 +338,7 @@
                     out[owner + pair * 4 + g, odd] = value.astype(jnp.bfloat16)
         return carry
 
-    lax.fori_loop(0, GROUP, give, 0)
+    lax.fori_loop(0, GROUP, give, 0, unroll=2)
 
 
 def rotated_planes(parts, fields, count):
@@ -390,8 +390,8 @@
     chunks = orbitals.reshape(2, block_count, OWN, NZ).swapaxes(0, 1)
     own = lax.all_to_all(chunks, BLOCKS, split_axis=0, concat_axis=0, tiled=True)
     def with_potential(field, v):
-        parts = [p.reshape(HALO * NY, NZ) for p in split_bf16(v)]
-        return jnp.concatenate([field.reshape(ROWS * HALO, NZ)] + parts, axis=0)
+        v = v.astype(jnp.bfloat16).reshape(HALO * NY, NZ)
+        return jnp.concatenate([field.reshape(ROWS * HALO, NZ), v], axis=0)
 
     tail = with_potential(own[:, :, OWN - HALO :], v_own[OWN - HALO :])
     head = with_potential(own[:, :, :HALO], v_own[:HALO])

time: 153 us -> 151 us (0.987)
  no operation moved by 1% of the time
where the time goes in v5:
time: 151 us; the launch traced here: 149 us
  blocking collectives  75.5 us (50%)
  starting transfers between devices  26.2 us (17%)
  Pallas kernels  20.7 us (14%)
  waiting for transfers between devices  20.2 us (13%)
  local copies, waits for them, and re-layouts  3.78 us (3%)
  between operations  2.21 us (1%)
    all_to_all x1, blocking collectives, local(): lax.all_to_all(rotated, ('l', 'h', 'y', 'x'), split_axis=0, concat_axis=0...  30.1 us
    all_to_all x1, blocking collectives, local(): lax.all_to_all(filtered, 'x', split_axis=0, concat_axis=0, tiled=True)  19.2 us
    all_to_all x1, waiting for transfers between devices, local(): lax.all_to_all(chunks, BLOCKS, split_axis=0, concat_axis=0, tiled=True)  14.9 us
    all_to_all x1, blocking collectives, local(): lax.all_to_all(sums, ('x', 'y'), split_axis=0, concat_axis=0, tiled=True)  13.5 us
    all_to_all x1, blocking collectives, local(): lax.all_to_all(sums, ('l', 'h'), split_axis=0, concat_axis=0, tiled=True)  12.7 us
    all_to_all x1, starting transfers between devices, local(): lax.all_to_all(chunks, BLOCKS, split_axis=0, concat_axis=0, tiled=True)  11.6 us
    ppermute x4, starting transfers between devices, local(): lax.ppermute(potential, ('x', 'y'), [(y * 4 + (x + j) % 4, x * 4 + y) for...  9.29 us
    pallas_call x1, Pallas kernels, inner_planes(): pl.pallas_call(inner_kernel, out_shape=(edge, edge, edge, jax.ShapeDtypeS...  7.21 us
  transfers between devices with their start and end apart: 7, of which 3 were waited for; matrix products, arithmetic and copies ran while one was open for 0% of the time, Pallas kernels for 5%

profile of v5, /device:TPU:2, one launch (start us, length us, event | category | flops | bytes accessed | tf_op | source)
XLA Modules:
  0.0 148.8 jit_solution(2851321225068812352)
XLA Ops:
  0.6 2.3 %copy.12 = bf16[2,32,64,128]{3,2,0,1:T(8,128)(2,1)} copy(bf16[2,32,64,128]{3,2,1,0:T(8,128)(2,1)} %bitcast.22) | data formatting | bytes 2097152 | tf_op jit(solution)/shard_map/reshape | solution.py:390
  2.9 0.0 copy-start.2
  2.9 11.6 %all-to-all-start = ((bf16[32,2,64,128]{3,2,1,0:T(8,128)(2,1)}), bf16[32,2,64,128]{3,2,1,0:T(8,128)(2,1)S(1)}, u32[]{:S(2)}, u32[]{:S(2)}) async-start(bf16[32,2,64,128]{3,2,1,0:T(8,128)(2,1)} %bitcast.17), calls=%async_computation | async-start | bytes 2097152 | tf_op jit(solution)/shard_map/all_to_all | solution.py:391
  14.5 0.0 copy-done.2
  14.6 3.4 %collective-permute-start = (f32[16,8,128]{2,1,0:T(8,128)S(1)}, f32[16,8,128]{2,1,0:T(8,128)S(1)}, u32[]{:S(2)}, u32[]{:S(2)}) collective-permute-start(f32[16,8,128]{2,1,0:T(8,128)S(1)} %copy-done.2), channel_id=1, source_target_pairs={{1,0},{33,1},{65,2},{97,3},{2,32},{34,33},{66,34},{98,35},{3,64},{... | collective-permute-start | bytes 196616 | tf_op jit(solution)/shard_map/ppermute | solution.py:378
  18.0 0.8 collective-permute-start.1
  18.8 5.0 %collective-permute-start.3 = (f32[16,8,128]{2,1,0:T(8,128)S(1)}, f32[16,8,128]{2,1,0:T(8,128)S(1)}, u32[]{:S(2)}, u32[]{:S(2)}) collective-permute-start(f32[16,8,128]{2,1,0:T(8,128)S(1)} %copy-done.2), channel_id=1, source_target_pairs={{0,0},{32,1},{64,2},{96,3},{1,32},{33,33},{65,34},{97,35},{2,64},{... | collective-permute-start | bytes 196616 | tf_op jit(solution)/shard_map/ppermute | solution.py:378
  23.8 0.1 collective-permute-start.2
  25.2 0.0 collective-permute-done
  25.2 0.0 collective-permute-done.1
  25.3 2.9 %collective-permute-done.2 = f32[16,8,128]{2,1,0:T(8,128)S(1)} collective-permute-done((f32[16,8,128]{2,1,0:T(8,128)S(1)}, f32[16,8,128]{2,1,0:T(8,128)S(1)}, u32[]{:S(2)}, u32[]{:S(2)}) %collective-permute-start.2) | collective-permute-done | bytes 65568 | tf_op jit(solution)/shard_map/ppermute | solution.py:378
  28.1 0.0 collective-permute-done.3.v
  28.2 14.9 %all-to-all-done = bf16[32,2,64,128]{3,2,1,0:T(8,128)(2,1)S(1)} async-done(((bf16[32,2,64,128]{3,2,1,0:T(8,128)(2,1)}), bf16[32,2,64,128]{3,2,1,0:T(8,128)(2,1)S(1)}, u32[]{:S(2)}, u32[]{:S(2)}) %all-to-all-start) | async-done | bytes 1048608 | tf_op jit(solution)/shard_map/all_to_all | solution.py:391
  43.2 0.1 fusion
  43.3 0.0 copy-start
  43.3 3.9 %collective-permute-start.4 = (bf16[1728,128]{1,0:T(8,128)(2,1)S(1)}, bf16[1728,128]{1,0:T(8,128)(2,1)S(1)}, u32[]{:S(2)}, u32[]{:S(2)}) collective-permute-start(bf16[1728,128]{1,0:T(8,128)(2,1)S(1)} %pad_maximum_fusion), channel_id=1, source_target_pairs={{0,4},{4,8},{8,12},{12,16},{16,20},{20,24},{24,28},{28,1},{1,5},{5... | collective-permute-start | bytes 1327112 | tf_op jit(solution)/shard_map/ppermute | solution.py:398
  47.2 1.5 collective-permute-start.5
  48.7 0.1 pad_maximum_fusion.2.scal
  48.8 0.1 pad_add_fusion.base
  48.9 0.0 copy-done
  48.9 7.2 %filter_inner.1 = (f32[2,12,64,128]{3,2,1,0:T(8,128)S(1)}, f32[2,12,64,128]{3,2,1,0:T(8,128)S(1)}, f32[2,12,64,128]{3,2,1,0:T(8,128)S(1)}, bf16[28,64,128]{2,1,0:T(8,128)(2,1)S(1)}) custom-call(f32[2]{0:T(128)S(1)} %pad_maximum_fusion.2.scal, bf16[4096,128]{1,0:T(8,128)(2,1)S(1)} %bitcast.18, f32[512,128]{1,0:T(8,128)S(1)} %dynamic-slice_bitcast_fusion.v_own, ...), custom_call_target="tpu_custom_call" | custom-call | flops 2000000000 | bytes 8000000 | tf_op jit(solution)/shard_map/filter_inner/pallas_call | solution.py:172
  56.1 0.0 collective-permute-done.4.left
  56.1 2.3 %collective-permute-done.5.right = bf16[1728,128]{1,0:T(8,128)(2,1)S(1)} collective-permute-done((bf16[1728,128]{1,0:T(8,128)(2,1)S(1)}, bf16[1728,128]{1,0:T(8,128)(2,1)S(1)}, u32[]{:S(2)}, u32[]{:S(2)}) %collective-permute-start.5) | collective-permute-done | bytes 442400 | tf_op jit(solution)/shard_map/ppermute | solution.py:399
  58.5 6.3 %filter_outer.1 = bf16[4,22,64,128]{3,2,1,0:T(8,128)(2,1)S(1)} custom-call(f32[2]{0:T(128)S(1)} %pad_maximum_fusion.2.scal, s32[2]{0:T(128)S(1)} %pad_add_fusion.base, bf16[1728,128]{1,0:T(8,128)(2,1)S(1)} %collective-permute-done.4.left, bf16[1728,128]{1,0:T(8,128)(2,1)S(1)} %collective-permute-done.5.right, ...), custom_call_target="tpu_custom_call" | custom-call | tf_op jit(solution)/shard_map/filter_outer/pallas_call | solution.py:197
  64.7 0.0 copy-start.1
  64.7 19.2 %all_to_all.25.planes = bf16[4,22,64,128]{3,2,1,0:T(8,128)(2,1)S(1)} all-to-all(bf16[4,22,64,128]{3,2,1,0:T(8,128)(2,1)S(1)} %filter_outer.1), channel_id=1, replica_groups=mesh['spin'=2,'x'=4,'h'=2,'l'=4,'y'=4] {'x'}, dimensions={0} | all-to-all | bytes 2883584 | tf_op jit(solution)/shard_map/all_to_all | solution.py:403
  84.0 0.0 copy-done.1
  84.0 2.6 %matrix_sums.1 = (f32[16,16,128]{2,1,0:T(8,128)S(1)}, bf16[16,32,1024]{2,1,0:T(8,128)(2,1)S(1)}) custom-call(bf16[4,22,64,128]{3,2,1,0:T(8,128)(2,1)S(1)} %all_to_all.25.planes, f32[16,8,128]{2,1,0:T(8,128)S(1)} %collective-permute-done.3.v, bf16[128,256]{1,0:T(8,128)(2,1)S(1)} %copy-done.1), custom_call_target="tpu_custom_call" | custom-call | tf_op jit(solution)/shard_map/matrix_sums/pallas_call | solution.py:271
  86.6 13.5 %all_to_all.26 = f32[16,16,128]{2,1,0:T(8,128)S(1)} all-to-all(f32[16,16,128]{2,1,0:T(8,128)S(1)} %get-tuple-element.14), channel_id=1, replica_groups=mesh['spin'=2,'x'=4,'h'=2,'l'=4,'y'=4] {'x','y'}, dimensions={0} | all-to-all | bytes 262144 | tf_op jit(solution)/shard_map/all_to_all | solution.py:405
  100.1 12.7 %all_to_all.27.refs_0_ = f32[8,16,128]{2,1,0:T(8,128)S(1)} all-to-all(f32[8,16,128]{2,1,0:T(8,128)S(1)} %broadcast_in_dim.2), channel_id=1, replica_groups=mesh['spin'=2,'x'=4,'h'=2,'l'=4,'y'=4] {'l','h'}, dimensions={0} | all-to-all | bytes 131072 | tf_op jit(solution)/shard_map/all_to_all | solution.py:407
  112.8 4.7 %rotate_planes.1 = (bf16[128,2,16,128]{3,2,1,0:T(8,128)(2,1)S(1)}, f32[32,32]{1,0:T(8,128)}) custom-call(f32[8,16,128]{2,1,0:T(8,128)S(1)} %all_to_all.27.refs_0_, bf16[16,32,1024]{2,1,0:T(8,128)(2,1)S(1)} %get-tuple-element.15.refs_1_), custom_call_target="tpu_custom_call" | custom-call | tf_op jit(solution)/shard_map/rotate_planes/pallas_call | solution.py:350
  117.5 30.1 %all_to_all.28 = bf16[128,2,16,128]{3,2,1,0:T(8,128)(2,1)S(1)} all-to-all(bf16[128,2,16,128]{3,2,1,0:T(8,128)(2,1)S(1)} %get-tuple-element.16), channel_id=1, replica_groups=mesh['spin'=2,'x'=4,'h'=2,'l'=4,'y'=4] {'l','h','y','x'}, dimensions={0} | all-to-all | bytes 2097152 | tf_op jit(solution)/shard_map/all_to_all | solution.py:409
  147.5 1.3 copy.10
  (14 shorter events, 0.2 us)
Async XLA Ops:
  2.9 11.6 %copy-start.2 = (f32[16,8,128]{2,1,0:T(8,128)S(1)}, f32[16,8,128]{2,1,0:T(8,128)}, u32[]{:S(2)}) copy-start(f32[16,8,128]{2,1,0:T(8,128)} %param.8) | copy-start | bytes 196612
  2.9 40.3 %all-to-all-start = ((bf16[32,2,64,128]{3,2,1,0:T(8,128)(2,1)}), bf16[32,2,64,128]{3,2,1,0:T(8,128)(2,1)S(1)}, u32[]{:S(2)}, u32[]{:S(2)}) async-start(bf16[32,2,64,128]{3,2,1,0:T(8,128)(2,1)} %bitcast.17), calls=%async_computation | async-start | bytes 2097152 | tf_op jit(solution)/shard_map/all_to_all | solution.py:391
  14.6 10.7 %collective-permute-start = (f32[16,8,128]{2,1,0:T(8,128)S(1)}, f32[16,8,128]{2,1,0:T(8,128)S(1)}, u32[]{:S(2)}, u32[]{:S(2)}) collective-permute-start(f32[16,8,128]{2,1,0:T(8,128)S(1)} %copy-done.2), channel_id=1, source_target_pairs={{1,0},{33,1},{65,2},{97,3},{2,32},{34,33},{66,34},{98,35},{3,64},{... | collective-permute-start | bytes 196616 | tf_op jit(solution)/shard_map/ppermute | solution.py:378
  18.0 7.2 %collective-permute-start.1 = (f32[16,8,128]{2,1,0:T(8,128)S(1)}, f32[16,8,128]{2,1,0:T(8,128)S(1)}, u32[]{:S(2)}, u32[]{:S(2)}) collective-permute-start(f32[16,8,128]{2,1,0:T(8,128)S(1)} %copy-done.2), channel_id=1, source_target_pairs={{2,0},{34,1},{66,2},{98,3},{3,32},{35,33},{67,34},{99,35},{0,64},{... | collective-permute-start | bytes 196616 | tf_op jit(solution)/shard_map/ppermute | solution.py:378
  18.8 9.4 %collective-permute-start.3 = (f32[16,8,128]{2,1,0:T(8,128)S(1)}, f32[16,8,128]{2,1,0:T(8,128)S(1)}, u32[]{:S(2)}, u32[]{:S(2)}) collective-permute-start(f32[16,8,128]{2,1,0:T(8,128)S(1)} %copy-done.2), channel_id=1, source_target_pairs={{0,0},{32,1},{64,2},{96,3},{1,32},{33,33},{65,34},{97,35},{2,64},{... | collective-permute-start | bytes 196616 | tf_op jit(solution)/shard_map/ppermute | solution.py:378
  23.8 4.3 %collective-permute-start.2 = (f32[16,8,128]{2,1,0:T(8,128)S(1)}, f32[16,8,128]{2,1,0:T(8,128)S(1)}, u32[]{:S(2)}, u32[]{:S(2)}) collective-permute-start(f32[16,8,128]{2,1,0:T(8,128)S(1)} %copy-done.2), channel_id=1, source_target_pairs={{3,0},{35,1},{67,2},{99,3},{0,32},{32,33},{64,34},{96,35},{1,64},{... | collective-permute-start | bytes 196616 | tf_op jit(solution)/shard_map/ppermute | solution.py:378
  43.3 5.6 %copy-start = (bf16[256,256]{1,0:T(8,128)(2,1)S(1)}, bf16[256,256]{1,0:T(8,128)(2,1)}, u32[]{:S(2)}) copy-start(bf16[256,256]{1,0:T(8,128)(2,1)} %constant.52.clone.kz) | copy-start | bytes 393220
  43.3 12.8 %collective-permute-start.4 = (bf16[1728,128]{1,0:T(8,128)(2,1)S(1)}, bf16[1728,128]{1,0:T(8,128)(2,1)S(1)}, u32[]{:S(2)}, u32[]{:S(2)}) collective-permute-start(bf16[1728,128]{1,0:T(8,128)(2,1)S(1)} %pad_maximum_fusion), channel_id=1, source_target_pairs={{0,4},{4,8},{8,12},{12,16},{16,20},{20,24},{24,28},{28,1},{1,5},{5... | collective-permute-start | bytes 1327112 | tf_op jit(solution)/shard_map/ppermute | solution.py:398
  47.2 11.2 %collective-permute-start.5 = (bf16[1728,128]{1,0:T(8,128)(2,1)S(1)}, bf16[1728,128]{1,0:T(8,128)(2,1)S(1)}, u32[]{:S(2)}, u32[]{:S(2)}) collective-permute-start(bf16[1728,128]{1,0:T(8,128)(2,1)S(1)} %pad_maximum_fusion.1), channel_id=1, source_target_pairs={{4,0},{8,4},{12,8},{16,12},{20,16},{24,20},{28,24},{1,28},{5,1},{9... | collective-permute-start | bytes 1327112 | tf_op jit(solution)/shard_map/ppermute | solution.py:399
  64.7 19.2 %copy-start.1 = (bf16[128,256]{1,0:T(8,128)(2,1)S(1)}, bf16[128,256]{1,0:T(8,128)(2,1)}, u32[]{:S(2)}) copy-start(bf16[128,256]{1,0:T(8,128)(2,1)} %constant.53.clone.kz) | copy-start | bytes 196612
